TPU v7x, 32 devices: a whole 2x2x4 slice. The times are simulated.
32 devices in a mesh: rep: 16 (over z, x, core), tp: 2 (over y).
Axes of the slice: x: 2, y: 2, z: 4, core: 2. Of those that a mesh axis runs over, the one named last changes fastest.
Arguments:
- hidden: bfloat16 [4, 1024, 8192], P(None, 'rep', 'tp'), may hold values from -6 to 6
- query_base: bfloat16 [4, 1024, 8192], P(None, 'rep', 'tp'), may hold values from -13 to 13
- kv_base: bfloat16 [4, 1024, 2, 1024], P(None, 'rep', None, 'tp'), may hold values from -6 to 6
- kv_cache: bfloat16 [1024, 128, 2, 1024], P('rep', None, None, 'tp'), may hold values from -13 to 13
- cache_lengths: int32 [1024], P('rep'), may hold values from 2 to 124
- adapter_ids: int32 [4, 1024], P(None, 'rep'), may hold values from 0 to 5, as said below
- migrating: int32 [4, 32], P(None, 'rep'), may hold values from 0 to 63, as said below
- pair_mask: int32 [4], replicated, may hold values from 1 to 8, as said below
- owners: int32 [4], replicated, may hold values from 0 to 15, as said below
- pool_down: bfloat16 [2, 2, 64, 8192], P(None, None, None, 'tp'), may hold values from -0.0625 to 0.0625
- pool_upq: bfloat16 [2, 64, 8192], P(None, None, 'tp'), may hold values from -0.75 to 0.75
- pool_upv: bfloat16 [2, 64, 1024], P(None, None, 'tp'), may hold values from -0.75 to 0.75
- store_down: bfloat16 [16, 2, 64, 8192], P('rep', None, None, 'tp'), may hold values from -0.0625 to 0.0625
- store_upq: bfloat16 [16, 64, 8192], P('rep', None, 'tp'), may hold values from -0.75 to 0.75
- store_upv: bfloat16 [16, 64, 1024], P('rep', None, 'tp'), may hold values from -0.75 to 0.75
Outputs:
- attention: bfloat16 [4, 1024, 8192], P(None, 'rep', 'tp')
Inputs may be any that keep to these rules, and one draw needn't show every extreme that they name: The 4 owners are distinct replicas. `migrating`: at one step the 2 entries of one replica are distinct slots. `adapter_ids`: at step s every entry is at most 2 + s. `pair_mask`: every entry is a power of two.
All inputs are finite; a program needn't handle non-finite values.
Results may differ from a plain program's by a relative error of at most 0.0064.
Values may be sent and summed in bfloat16 or wider, within the bound.
A program may use at most 256 MiB of HBM per device.

v0:
```python
from functools import partial
import math

import jax
import jax.numpy as jnp
from jax import lax
from jax.sharding import PartitionSpec as P

HD = 128
POOL = 2
STEPS = 4


def for_sending(value):

    def short(part):
        return part.astype(jnp.bfloat16) if part.dtype == jnp.float32 else part

    return jax.tree.map(short, value)


def swapped(value, axis, bit):
    mask = 2**bit
    pairs = [(source, source ^ mask) for source in range(lax.axis_size(axis))]
    return lax.ppermute(value, axis, pairs)


def from_root(value, axis, source):
    kept = jnp.where(lax.axis_index(axis) == source, value, 0).astype(value.dtype)
    return lax.psum(kept, axis)


def attend(query_rows, kv_rows, lengths, head_dim):
    req_count = kv_rows.shape[0]
    ctx_len = kv_rows.shape[1]
    kv_local = kv_rows.shape[3] // head_dim
    group_size = query_rows.shape[1] // (kv_local * head_dim)
    heads_q = query_rows.reshape(req_count, kv_local, group_size, head_dim)
    key_rows = kv_rows[:, :, 0].reshape(req_count, ctx_len, kv_local, head_dim)
    value_rows = kv_rows[:, :, 1].reshape(req_count, ctx_len, kv_local, head_dim)
    scores = jnp.einsum(
        "rkgd,rckd->rkgc", heads_q, key_rows, preferred_element_type=jnp.float32
    ) / math.sqrt(head_dim)
    valid_mask = jnp.arange(ctx_len)[None, :] <= lengths[:, None]
    scores = jnp.where(valid_mask[:, None, None, :], scores, -1e30)
    row_peak = jnp.max(scores, axis=-1, keepdims=True)
    exp_scores = jnp.exp(scores - row_peak)
    weights = (exp_scores / jnp.sum(exp_scores, axis=-1, keepdims=True)).astype(jnp.bfloat16)
    mixed_out = jnp.einsum(
        "rkgc,rckd->rkgd", weights, value_rows, preferred_element_type=jnp.float32
    )
    return mixed_out.astype(jnp.bfloat16).reshape(req_count, -1)


def cross_bit(bit_num, operand):
    return jax.tree.map(
        lambda part, own: part.astype(own.dtype),
        swapped(for_sending(operand), "rep", bit_num),
        operand,
    )


def local(
    hidden,
    query_base,
    kv_base,
    kv_cache,
    cache_lengths,
    adapter_ids,
    migrating,
    pair_mask,
    owners,
    pool_down,
    pool_upq,
    pool_upv,
    store_down,
    store_upq,
    store_upv,
):
    slots_all = POOL + STEPS
    down_all = jnp.concatenate(
        [pool_down, jnp.zeros((STEPS,) + pool_down.shape[1:], jnp.bfloat16)], axis=0
    )
    upq_all = jnp.concatenate(
        [pool_upq, jnp.zeros((STEPS,) + pool_upq.shape[1:], jnp.bfloat16)], axis=0
    )
    upv_all = jnp.concatenate(
        [pool_upv, jnp.zeros((STEPS,) + pool_upv.shape[1:], jnp.bfloat16)], axis=0
    )
    kv_state = kv_cache
    lengths = cache_lengths
    req_count = kv_cache.shape[0]
    bit_total = lax.axis_size("rep").bit_length() - 1
    outputs = []
    for step_num in range(STEPS):
        arrived = (
            from_root(store_down[0], "rep", owners[step_num]),
            from_root(store_upq[0], "rep", owners[step_num]),
            from_root(store_upv[0], "rep", owners[step_num]),
        )
        down_all = down_all.at[POOL + step_num].set(arrived[0])
        upq_all = upq_all.at[POOL + step_num].set(arrived[1])
        upv_all = upv_all.at[POOL + step_num].set(arrived[2])
        slot_ids = migrating[step_num]
        moving = kv_state[slot_ids]
        moving_len = lengths[slot_ids].astype(jnp.bfloat16)
        which_bit = jnp.zeros((), jnp.int32)
        for bit_num in range(bit_total):
            which_bit = which_bit + jnp.where(
                pair_mask[step_num] == 1 << bit_num, bit_num, 0
            ).astype(jnp.int32)
        branch_list = [partial(cross_bit, bit_num) for bit_num in range(bit_total)]
        moving, moving_len = lax.switch(which_bit, branch_list, (moving, moving_len))
        kv_state = kv_state.at[slot_ids].set(moving)
        lengths = lengths.at[slot_ids].set(moving_len.astype(jnp.int32))
        tokens = hidden[step_num]
        partial_sum = jnp.einsum(
            "rd,apkd->rapk", tokens, down_all, preferred_element_type=jnp.float32
        )
        picker = (adapter_ids[step_num][:, None] == jnp.arange(slots_all)[None, :]).astype(
            jnp.float32
        )
        summed = lax.psum(partial_sum, "tp")
        low_rank = jnp.sum(picker[:, :, None, None] * summed, axis=1)
        low_rank = low_rank.astype(jnp.bfloat16)
        spread = picker.astype(jnp.bfloat16)[:, :, None, None] * low_rank[:, None]
        spread_q = spread[:, :, 0].reshape(req_count, -1)
        spread_v = spread[:, :, 1].reshape(req_count, -1)
        delta_q = jnp.dot(
            spread_q, upq_all.reshape(-1, upq_all.shape[2]), preferred_element_type=jnp.float32
        )
        delta_v = jnp.dot(
            spread_v, upv_all.reshape(-1, upv_all.shape[2]), preferred_element_type=jnp.float32
        )
        query_rows = (query_base[step_num].astype(jnp.float32) + delta_q).astype(jnp.bfloat16)
        new_value = (kv_base[step_num][:, 1].astype(jnp.float32) + delta_v).astype(jnp.bfloat16)
        fresh_rows = jnp.stack([kv_base[step_num][:, 0], new_value], axis=1)
        kv_state = kv_state.at[jnp.arange(req_count), lengths].set(fresh_rows)
        outputs.append(attend(query_rows, kv_state, lengths, HD))
        lengths = lengths + 1
    return jnp.stack(outputs, axis=0)


def solution(mesh):
    return jax.shard_map(
        local,
        mesh=mesh,
        in_specs=(
            P(None, "rep", "tp"),
            P(None, "rep", "tp"),
            P(None, "rep", None, "tp"),
            P("rep", None, None, "tp"),
            P("rep"),
            P(None, "rep"),
            P(None, "rep"),
            P(),
            P(),
            P(None, None, None, "tp"),
            P(None, None, "tp"),
            P(None, None, "tp"),
            P("rep", None, None, "tp"),
            P("rep", None, "tp"),
            P("rep", None, "tp"),
        ),
        out_specs=P(None, "rep", "tp"),
        check_vma=False,
    )
```

profile of v0, /device:TPU:0, one launch (start us, length us, event | category | flops | bytes accessed | tf_op | source)
XLA Modules:
  0.0 1055.7 jit_solution(1297638653101811571)
XLA Ops:
  7.2 14.2 %copy.224 = bf16[64,128,2,512]{3,2,1,0:T(2,128)(2,1)} copy(bf16[64,128,2,512]{3,2,1,0:T(2,128)(2,1)} %param.58) | data formatting | bytes 33554432
  48.8 47.0 %conditional.16 = (bf16[2,128,2,512]{3,2,1,0:T(2,128)(2,1)}, bf16[2]{0:T(256)(128)(2,1)}) conditional(s32[]{:T(128)} %bitcast.17, (bf16[64,128,2,512]{3,2,1,0:T(2,128)(2,1)}, s32[2,1]{0,1:T(1,128)S(1)}, bf16[2]{0:T(256)(128)(2,1)S(1)}) %tuple.189, (bf16[64,128,2,512]{3,2,1,0:T(2,128)(2,1)}, s32[2,1]{0,1:T(1,128)S(1)}, ...), branch_computations={%region_0.1_spmd, %region_1.2_spmd, %region_2.3_spmd, %region_3.4_... | conditional | flops 1024 | bytes 3149952
  60.6 35.1 %collective-permute-done.7 = bf16[2]{0:T(256)(128)(2,1)} collective-permute-done((bf16[2]{0:T(256)(128)(2,1)S(1)}, bf16[2]{0:T(256)(128)(2,1)}, u32[]{:S(2)}, u32[]{:S(2)}) %collective-permute-start.7) | collective-permute-done | bytes 36 | tf_op jit(solution)/shard_map/cond/branch_3_fun/ppermute | solution.py:25
  122.0 80.5 %all-reduce.10.cloned.1.call-done = (bf16[1,2,64,4096]{3,2,1,0:T(8,128)(2,1)}, bf16[1,2,64,4096]{3,2,1,0:T(8,128)(2,1)}, bf16[1,2,64,4096]{3,2,1,0:T(8,128)(2,1)...) async-done(((bf16[1,2,64,4096]{3,2,1,0:T(8,128)(2,1)}, ...) | async-done | bytes 6553616 | tf_op jit(solution)/shard_map/psum | solution.py:30
  231.7 50.3 %all-reduce.8.cloned.1.call-done = (f32[64,6,2,64]{0,3,2,1:T(8,128)}, f32[64,6,2,64]{0,3,2,1:T(8,128)}, f32[64,6,2,64]{0,3,2,1:T(8,128)}, f32[64,6,2,64]{0,3,2,1:T(8,128)}) async-done(((f32[64,6,2,64]{0,3,2,1:T(8,128)}, f32[64,6,2,64]{0,3,2,1:T(8,128)}, f32[64,6,2,64]{0,3,2,1:T(8,128)}, f32[64,6,2,64]{0,3,2,1:T(8,128)}), (f32[64,6,2,64]{0,3,2,1:T(8,128)}, f32[64,6,2,64]{0,3,2,1:T(8,128)}, ...) | async-done | bytes 786448 | tf_op jit(solution)/shard_map/psum | solution.py:123
  299.8 32.6 %fusion.69 = (bf16[64,128,1,512]{3,2,1,0:T(2,128)(2,1)}, bf16[64,128,1,512]{3,2,1,0:T(2,128)(2,1)}) fusion(bf16[64,128,2,512]{3,2,1,0:T(2,128)(2,1)} %scatter_fusion.2), kind=kLoop, calls=%fused_computation.227 | loop fusion | bytes 33554432 | tf_op jit(solution)/shard_map/slice | solution.py:39
  332.4 15.8 %copy.83 = bf16[64,128,2,512]{3,1,2,0:T(8,128)(2,1)} copy(bf16[64,128,2,512]{3,2,1,0:T(2,128)(2,1)} %scatter_fusion.2) | data formatting | bytes 33554432 | tf_op jit(solution)/shard_map/scatter | solution.py:138
  364.5 30.7 %copy.86 = bf16[64,128,2,512]{3,2,1,0:T(2,128)(2,1)} copy(bf16[64,128,2,512]{3,1,2,0:T(8,128)(2,1)} %scatter_fusion.4) | data formatting | bytes 33554432 | tf_op jit(solution)/shard_map/scatter | solution.py:114
  412.0 32.7 %fusion.70 = (bf16[64,128,1,512]{3,2,1,0:T(2,128)(2,1)}, bf16[64,128,1,512]{3,2,1,0:T(2,128)(2,1)}) fusion(bf16[64,128,2,512]{3,2,1,0:T(2,128)(2,1)} %scatter_fusion.5), kind=kLoop, calls=%fused_computation.228 | loop fusion | bytes 33554432 | tf_op jit(solution)/shard_map/slice | solution.py:39
  455.1 35.2 %conditional.14 = (s32[2]{0:T(128)S(1)}, bf16[2,128,2,512]{3,1,2,0:T(8,128)(2,1)S(1)}) conditional(s32[]{:T(128)} %bitcast.53, (bf16[64,128,2,512]{3,2,1,0:T(2,128)(2,1)}, s32[2,1]{0,1:T(1,128)S(1)}, bf16[2]{0:T(256)(128)(2,1)}) %tuple.316, (bf16[64,128,2,512]{3,2,1,0:T(2,128)(2,1)}, s32[2,1]{0,1:T(1,128)S(1)}, ...), branch_computations={%region_28.29_spmd, %region_29.30_spmd, %region_30.31_spmd, %regio... | conditional | flops 1026 | bytes 4198540
  466.9 23.4 %collective-permute-done.23 = bf16[2]{0:T(256)(128)(2,1)S(1)} collective-permute-done((bf16[2]{0:T(256)(128)(2,1)}, bf16[2]{0:T(256)(128)(2,1)S(1)}, u32[]{:S(2)}, u32[]{:S(2)}) %collective-permute-start.23) | collective-permute-done | bytes 36 | tf_op jit(solution)/shard_map/cond/branch_3_fun/ppermute | solution.py:25
  505.4 30.7 %copy.97 = bf16[64,128,2,512]{3,2,1,0:T(2,128)(2,1)} copy(bf16[64,128,2,512]{3,1,2,0:T(8,128)(2,1)} %scatter_fusion.7) | data formatting | bytes 33554432 | tf_op jit(solution)/shard_map/scatter | solution.py:114
  544.6 32.6 %fusion.71 = (bf16[64,128,1,512]{3,2,1,0:T(2,128)(2,1)}, bf16[64,128,1,512]{3,2,1,0:T(2,128)(2,1)}) fusion(bf16[64,128,2,512]{3,2,1,0:T(2,128)(2,1)} %scatter_fusion.8), kind=kLoop, calls=%fused_computation.229 | loop fusion | bytes 33554432 | tf_op jit(solution)/shard_map/slice | solution.py:39
  586.4 21.4 %conditional.15 = (s32[2]{0:T(128)S(1)}, bf16[2,128,2,512]{3,1,2,0:T(8,128)(2,1)S(1)}) conditional(s32[]{:T(128)} %bitcast.71, (bf16[64,128,2,512]{3,2,1,0:T(2,128)(2,1)}, s32[2,1]{0,1:T(1,128)S(1)}, bf16[2]{0:T(256)(128)(2,1)}) %tuple.308, (bf16[64,128,2,512]{3,2,1,0:T(2,128)(2,1)}, s32[2,1]{0,1:T(1,128)S(1)}, ...), branch_computations={%region_42.43_spmd, %region_43.44_spmd, %region_44.45_spmd, %regio... | conditional | flops 1026 | bytes 4198540
  610.0 33.2 %copy.77 = bf16[64,128,1,512]{1,3,0,2:T(8,128)(2,1)} copy(bf16[64,128,1,512]{3,2,1,0:T(2,128)(2,1)} %get-tuple-element.411) | data formatting | bytes 16777216 | tf_op jit(solution)/shard_map/slice | solution.py:39
  647.6 33.2 %copy.79 = bf16[64,128,1,512]{1,3,0,2:T(8,128)(2,1)} copy(bf16[64,128,1,512]{3,2,1,0:T(2,128)(2,1)} %get-tuple-element.412) | data formatting | bytes 16777216 | tf_op jit(solution)/shard_map/slice | solution.py:40
  699.4 33.2 %copy.88 = bf16[64,128,1,512]{1,3,0,2:T(8,128)(2,1)} copy(bf16[64,128,1,512]{3,2,1,0:T(2,128)(2,1)} %get-tuple-element.413) | data formatting | bytes 16777216 | tf_op jit(solution)/shard_map/slice | solution.py:39
  738.0 33.6 %copy.90 = bf16[64,128,1,512]{1,3,0,2:T(8,128)(2,1)} copy(bf16[64,128,1,512]{3,2,1,0:T(2,128)(2,1)} %get-tuple-element.414) | data formatting | bytes 16777216 | tf_op jit(solution)/shard_map/slice | solution.py:40
  790.1 33.2 %copy.99 = bf16[64,128,1,512]{1,3,0,2:T(8,128)(2,1)} copy(bf16[64,128,1,512]{3,2,1,0:T(2,128)(2,1)} %get-tuple-element.415) | data formatting | bytes 16777216 | tf_op jit(solution)/shard_map/slice | solution.py:39
  828.7 33.2 %copy.101 = bf16[64,128,1,512]{1,3,0,2:T(8,128)(2,1)} copy(bf16[64,128,1,512]{3,2,1,0:T(2,128)(2,1)} %get-tuple-element.416) | data formatting | bytes 16777216 | tf_op jit(solution)/shard_map/slice | solution.py:40
  883.2 30.8 %copy.108 = bf16[64,128,2,512]{3,2,1,0:T(2,128)(2,1)} copy(bf16[64,128,2,512]{3,1,2,0:T(8,128)(2,1)} %scatter_fusion.10) | data formatting | bytes 33554432 | tf_op jit(solution)/shard_map/scatter | solution.py:114
  929.8 32.6 %fusion.72 = (bf16[64,128,1,512]{3,2,1,0:T(2,128)(2,1)}, bf16[64,128,1,512]{3,2,1,0:T(2,128)(2,1)}) fusion(bf16[64,128,2,512]{3,2,1,0:T(2,128)(2,1)} %scatter_fusion.11), kind=kLoop, calls=%fused_computation.230 | loop fusion | bytes 33554432 | tf_op jit(solution)/shard_map/slice | solution.py:39
  962.5 33.3 %copy.110 = bf16[64,128,1,512]{1,3,0,2:T(8,128)(2,1)} copy(bf16[64,128,1,512]{3,2,1,0:T(2,128)(2,1)} %get-tuple-element.417) | data formatting | bytes 16777216 | tf_op jit(solution)/shard_map/slice | solution.py:39
  998.8 33.2 %copy.112 = bf16[64,128,1,512]{1,3,0,2:T(8,128)(2,1)} copy(bf16[64,128,1,512]{3,2,1,0:T(2,128)(2,1)} %get-tuple-element.418) | data formatting | bytes 16777216 | tf_op jit(solution)/shard_map/slice | solution.py:40
  (238 shorter events, 333.9 us)
Async XLA Ops:
  6.5 196.0 %all-reduce.10.cloned.1.call-start = ((), (), s32[]{:S(2)}) async-start(), calls=%async_computation.1 | async-start | bytes 13107200 | tf_op jit(solution)/shard_map/psum | solution.py:30
  7.2 17.4 %copy-start.9 = (bf16[1,2,64,4096]{3,2,1,0:T(8,128)(2,1)S(1)}, bf16[1,2,64,4096]{3,2,1,0:T(8,128)(2,1)}, u32[]{:S(2)}) copy-start(bf16[1,2,64,4096]{3,2,1,0:T(8,128)(2,1)} %param.67) | copy-start | bytes 3145732
  7.2 21.9 %copy-start.18 = (bf16[1,64,512]{2,1,0:T(8,128)(2,1)S(1)}, bf16[1,64,512]{2,1,0:T(8,128)(2,1)}, u32[]{:S(2)}) copy-start(bf16[1,64,512]{2,1,0:T(8,128)(2,1)} %param.69) | copy-start | bytes 196612
  21.4 17.0 %copy-start.32 = (s32[4,64]{1,0:T(4,128)S(1)}, s32[4,64]{1,0:T(4,128)}, u32[]{:S(2)}) copy-start(s32[4,64]{1,0:T(4,128)} %param.60) | copy-start | bytes 3076
  21.4 18.9 %copy-start.5 = (bf16[2,2,64,4096]{3,2,1,0:T(8,128)(2,1)S(1)}, bf16[2,2,64,4096]{3,2,1,0:T(8,128)(2,1)}, u32[]{:S(2)}) copy-start(bf16[2,2,64,4096]{3,2,1,0:T(8,128)(2,1)} %param.64) | copy-start | bytes 6291460
  26.7 17.1 %copy-start.17 = (bf16[2,64,512]{2,1,0:T(8,128)(2,1)S(1)}, bf16[2,64,512]{2,1,0:T(8,128)(2,1)}, u32[]{:S(2)}) copy-start(bf16[2,64,512]{2,1,0:T(8,128)(2,1)} %param.66) | copy-start | bytes 393220
  29.8 17.0 %copy-start.20 = (s32[4,2]{0,1:T(2,128)S(1)}, s32[4,2]{0,1:T(2,128)}, u32[]{:S(2)}) copy-start(s32[4,2]{0,1:T(2,128)} %param.61) | copy-start | bytes 100
  29.9 252.2 %all-reduce.8.cloned.1.call-start = ((), (), s32[]{:S(2)}) async-start(), calls=%async_computation | async-start | bytes 3145728 | tf_op jit(solution)/shard_map/psum | solution.py:123
  48.1 70.3 %copy-start.26 = (s32[2]{0:T(128)}, s32[2]{0:T(128)S(1)}, u32[]{:S(2)}) copy-start(s32[2]{0:T(128)S(1)} %get-tuple-element.462) | copy-start | bytes 28
  56.4 39.4 %collective-permute-start.6 = (bf16[2,128,2,512]{3,2,1,0:T(2,128)(2,1)S(1)}, bf16[2,128,2,512]{3,2,1,0:T(2,128)(2,1)}, u32[]{:S(2)}, u32[]{:S(2)}) collective-permute-start(bf16[2,128,2,512]{3,2,1,0:T(2,128)(2,1)S(1)} %gather_fusion.3), channel_id=1, source_target_pairs={{0,16},{2,18},{4,20},{6,22},{8,24},{10,26},{12,28},{14,30},{16,0},... | collective-permute-start | bytes 1572872 | tf_op jit(solution)/shard_map/cond/branch_3_fun/ppermute | solution.py:25
  60.6 35.2 %collective-permute-start.7 = (bf16[2]{0:T(256)(128)(2,1)S(1)}, bf16[2]{0:T(256)(128)(2,1)}, u32[]{:S(2)}, u32[]{:S(2)}) collective-permute-start(bf16[2]{0:T(256)(128)(2,1)S(1)} %get-tuple-element.304), channel_id=1, source_target_pairs={{0,16},{2,18},{4,20},{6,22},{8,24},{10,26},{12,28},{14,30},{16,0},... | collective-permute-start | bytes 20 | tf_op jit(solution)/shard_map/cond/branch_3_fun/ppermute | solution.py:25
  119.6 97.3 %copy-start.24 = (s32[2]{0:T(128)}, s32[2]{0:T(128)S(1)}, u32[]{:S(2)}) copy-start(s32[2]{0:T(128)S(1)} %get-tuple-element.450) | copy-start | bytes 28
  357.1 2.1 collective-permute-start.8
  357.1 2.1 collective-permute-start.9
  412.0 32.7 %copy-start = (bf16[64,128,2,512]{3,2,1,0:T(2,128)(2,1)S(1)}, bf16[64,128,2,512]{3,2,1,0:T(2,128)(2,1)}, u32[]{:S(2)}) copy-start(bf16[64,128,2,512]{3,2,1,0:T(2,128)(2,1)} %scatter_fusion.5) | copy-start | bytes 50331652
  452.5 38.7 %copy-start.29 = (s32[2]{0:T(128)S(1)}, s32[2]{0:T(128)}, u32[]{:S(2)}) copy-start(s32[2]{0:T(128)} %copy-done.28) | copy-start | bytes 28
  464.0 26.3 %collective-permute-start.22 = (bf16[2,128,2,512]{3,2,1,0:T(2,128)(2,1)}, bf16[2,128,2,512]{3,2,1,0:T(2,128)(2,1)S(1)}, u32[]{:S(2)}, u32[]{:S(2)}) collective-permute-start(bf16[2,128,2,512]{3,2,1,0:T(2,128)(2,1)} %gather_fusion.11), channel_id=1, source_target_pairs={{0,16},{2,18},{4,20},{6,22},{8,24},{10,26},{12,28},{14,30},{16,0},... | collective-permute-start | bytes 1572872 | tf_op jit(solution)/shard_map/cond/branch_3_fun/ppermute | solution.py:25
  466.4 23.9 %collective-permute-start.23 = (bf16[2]{0:T(256)(128)(2,1)}, bf16[2]{0:T(256)(128)(2,1)S(1)}, u32[]{:S(2)}, u32[]{:S(2)}) collective-permute-start(bf16[2]{0:T(256)(128)(2,1)} %get-tuple-element.328), channel_id=1, source_target_pairs={{0,16},{2,18},{4,20},{6,22},{8,24},{10,26},{12,28},{14,30},{16,0},... | collective-permute-start | bytes 20 | tf_op jit(solution)/shard_map/cond/branch_3_fun/ppermute | solution.py:25
  544.6 32.6 %copy-start.1 = (bf16[64,128,2,512]{3,2,1,0:T(2,128)(2,1)S(1)}, bf16[64,128,2,512]{3,2,1,0:T(2,128)(2,1)}, u32[]{:S(2)}) copy-start(bf16[64,128,2,512]{3,2,1,0:T(2,128)(2,1)} %scatter_fusion.8) | copy-start | bytes 50331652
  585.0 23.7 %copy-start.25 = (s32[2]{0:T(128)S(1)}, s32[2]{0:T(128)}, u32[]{:S(2)}) copy-start(s32[2]{0:T(128)} %copy-done.24) | copy-start | bytes 28
  594.6 13.2 %collective-permute-start.26 = (bf16[2,128,2,512]{3,2,1,0:T(2,128)(2,1)}, bf16[2,128,2,512]{3,2,1,0:T(2,128)(2,1)S(1)}, u32[]{:S(2)}, u32[]{:S(2)}) collective-permute-start(bf16[2,128,2,512]{3,2,1,0:T(2,128)(2,1)} %gather_fusion.13), channel_id=1, source_target_pairs={{0,4},{2,6},{4,0},{6,2},{8,12},{10,14},{12,8},{14,10},{16,20},{18,... | collective-permute-start | bytes 1572872 | tf_op jit(solution)/shard_map/cond/branch_1_fun/ppermute | solution.py:25
  596.2 11.6 %collective-permute-start.27 = (bf16[2]{0:T(256)(128)(2,1)}, bf16[2]{0:T(256)(128)(2,1)S(1)}, u32[]{:S(2)}, u32[]{:S(2)}) collective-permute-start(bf16[2]{0:T(256)(128)(2,1)} %get-tuple-element.334), channel_id=1, source_target_pairs={{0,4},{2,6},{4,0},{6,2},{8,12},{10,14},{12,8},{14,10},{16,20},{18,... | collective-permute-start | bytes 20 | tf_op jit(solution)/shard_map/cond/branch_1_fun/ppermute | solution.py:25
  962.5 33.3 %copy-start.16 = (bf16[64,6,1,64]{3,1,0,2:T(8,128)(2,1)S(1)}, bf16[64,6,1,64]{3,1,0,2:T(8,128)(2,1)}, u32[]{:S(2)}) copy-start(bf16[64,6,1,64]{3,1,0,2:T(8,128)(2,1)} %get-tuple-element.437) | copy-start | bytes 147460
  998.8 33.2 %copy-start.19 = (pred[64,128]{1,0:T(8,128)(4,1)S(1)}, pred[64,128]{1,0:T(8,128)(4,1)}, u32[]{:S(2)}) copy-start(pred[64,128]{1,0:T(8,128)(4,1)} %iota_compare_fusion) | copy-start | bytes 24580
  (20 other events, 175.2 us)
Sparse Core Ops, SparseCore 0:
  30.0 172.4 all-reduce.9
  229.9 52.0 all-reduce.7
where the time goes:
time: 1070 us; the launch traced here: 1060 us
  local copies, waits for them, and re-layouts  691 us (65%)
  waiting for transfers between devices  202 us (19%)
  matrix products  96 us (9%)
  other arithmetic  32.3 us (3%)
  between operations  24.5 us (2%)
    slice x8, local copies, waits for them, and re-layouts, attend(): key_rows = kv_rows[:, :, 0].reshape(req_count, ctx_len, kv_local, head_dim)  264 us
    slice x4, local copies, waits for them, and re-layouts, attend(): kv_rows[:, :, 1].reshape(req_count, ctx_len, kv_local, head_dim)  133 us
    scatter x7, local copies, waits for them, and re-layouts, local(): kv_state = kv_state.at[slot_ids].set(moving)  105 us
    psum x1, waiting for transfers between devices, from_root(): return lax.psum(kept, axis)  80.5 us
    ppermute x8, waiting for transfers between devices, swapped(): return lax.ppermute(value, axis, pairs)  71.3 us
    scatter x7, local copies, waits for them, and re-layouts, local(): kv_state = kv_state.at[jnp.arange(req_count), lengths].set(fresh_rows)  65 us
    psum x1, waiting for transfers between devices, local(): summed = lax.psum(partial_sum, 'tp')  50.3 us
    dot_general x4, matrix products, attend(): jnp.einsum('rkgc,rckd->rkgd', weights, value_rows, preferred_element_type...  35.9 us
  transfers between devices with their start and end apart: 10, of which 6 were waited for; matrix products, arithmetic and copies ran while one was open for 4% of the time, Pallas kernels for 0%

commit v1 on v0

v1 whole, which is shorter than its diff:
```python
from functools import partial
import math

import jax
import jax.numpy as jnp
from jax import lax
from jax.experimental import pallas as pl
from jax.experimental.pallas import tpu as pltpu
from jax.sharding import PartitionSpec as P

HD = 128
LANES = 128


def swapped(value, axis, bit):
    mask = 2**bit
    pairs = [(source, source ^ mask) for source in range(lax.axis_size(axis))]
    return lax.ppermute(value, axis, pairs)


def bit_of(mask, bit_total):
    which = jnp.zeros((), jnp.int32)
    for bit in range(bit_total):
        which = which + jnp.where(mask == 1 << bit, bit, 0).astype(jnp.int32)
    return which


def exchange(value, which, bit_total):
    branches = [lambda part, bit=bit: swapped(part, "rep", bit) for bit in range(bit_total)]
    return lax.switch(which, branches, value)


def attend_kernel(group, lens_ref, query_ref, fresh_ref, cache_ref, out_ref):
    base = pl.program_id(0) * query_ref.shape[0]
    rows, span = query_ref.shape[2], 2 * cache_ref.shape[1]
    extra = fresh_ref.shape[2] // 2
    col = lax.broadcasted_iota(jnp.int32, (1, span), 1)
    is_key = col % 2 == 0
    place = col // 2
    col_new = lax.broadcasted_iota(jnp.int32, (rows, extra), 1)
    step_of = lax.broadcasted_iota(jnp.int32, (rows, extra), 0) // group
    seen_new = col_new <= step_of
    scale = 1.0 / math.sqrt(HD)
    contract = (((1,), (1,)), ((), ()))
    for r in range(query_ref.shape[0]):
        both = cache_ref.at[r, :, 0].reshape(span, HD)[...]
        query = query_ref[r, 0]
        key_new, value_new = fresh_ref[r, 0, :extra], fresh_ref[r, 0, extra:]
        old = lax.dot_general(query, both, contract, preferred_element_type=jnp.float32)
        new = lax.dot_general(query, key_new, contract, preferred_element_type=jnp.float32)
        seen = is_key & (place < lens_ref[base + r])
        old = jnp.where(seen, old * scale, -1e30)
        new = jnp.where(seen_new, new * scale, -1e30)
        peak = jnp.maximum(
            jnp.max(old, axis=1, keepdims=True), jnp.max(new, axis=1, keepdims=True)
        )
        old, new = jnp.exp(old - peak), jnp.exp(new - peak)
        total = jnp.sum(old, axis=1, keepdims=True) + jnp.sum(new, axis=1, keepdims=True)
        part = 1.0 / total
        old = pltpu.roll(old * part, 1, 1).astype(jnp.bfloat16)
        new = (new * part).astype(jnp.bfloat16)
        mixed = jnp.dot(old, both, preferred_element_type=jnp.float32)
        mixed = mixed + jnp.dot(new, value_new, preferred_element_type=jnp.float32)
        out_ref[r, 0] = mixed.astype(out_ref.dtype)


def attend(query, new_key, new_value, kv_cache, lengths):
    steps, reqs = query.shape[:2]
    ctx = kv_cache.shape[1]
    heads = kv_cache.shape[3] // HD
    group = query.shape[2] // (heads * HD)
    rows = steps * group
    query = query.reshape(steps, reqs, heads, group, HD).transpose(1, 2, 0, 3, 4)
    query = query.reshape(reqs, heads, rows, HD)
    extra = -(-steps // 16) * 16
    fresh = jnp.stack([new_key, new_value]).reshape(2, steps, reqs, heads, HD)
    fresh = jnp.pad(fresh.transpose(2, 3, 0, 1, 4), ((0, 0),) * 3 + ((0, extra - steps), (0, 0)))
    fresh = fresh.reshape(reqs, heads, 2 * extra, HD)
    cache = kv_cache.reshape(reqs, ctx, 2, heads, HD).transpose(0, 1, 3, 2, 4)
    many = 8 if reqs % 8 == 0 else 1
    out = pl.pallas_call(
        partial(attend_kernel, group),
        grid=(reqs // many, heads),
        in_specs=[
            pl.BlockSpec(memory_space=pltpu.SMEM),
            pl.BlockSpec((many, 1, rows, HD), lambda r, h: (r, h, 0, 0)),
            pl.BlockSpec((many, 1, 2 * extra, HD), lambda r, h: (r, h, 0, 0)),
            pl.BlockSpec((many, ctx, 1, 2, HD), lambda r, h: (r, 0, h, 0, 0)),
        ],
        out_specs=pl.BlockSpec((many, 1, rows, HD), lambda r, h: (r, h, 0, 0)),
        out_shape=jax.ShapeDtypeStruct((reqs, heads, rows, HD), jnp.bfloat16),
        compiler_params=pltpu.CompilerParams(vmem_limit_bytes=24 << 20),
        cost_estimate=pl.CostEstimate(
            flops=8 * reqs * heads * rows * ctx * HD,
            bytes_accessed=2 * kv_cache.size,
            transcendentals=2 * reqs * heads * rows * ctx,
        ),
        name="attend",
    )(lengths, query, fresh, cache)
    out = out.reshape(reqs, heads, steps, group, HD).transpose(2, 0, 1, 3, 4)
    return out.reshape(steps, reqs, -1)


def local(
    hidden,
    query_base,
    kv_base,
    kv_cache,
    cache_lengths,
    adapter_ids,
    migrating,
    pair_mask,
    owners,
    pool_down,
    pool_upq,
    pool_upv,
    store_down,
    store_upq,
    store_upv,
):
    steps, reqs, width = hidden.shape
    kv_width = kv_base.shape[3]
    pool = pool_down.shape[0]
    slots = pool + steps
    bit_total = lax.axis_size("rep").bit_length() - 1
    me = lax.axis_index("rep")

    mine = (owners == me)[:, None]
    flat = jnp.concatenate([store_down[0].reshape(-1, width), store_upq[0]], axis=0)
    sent = jnp.where(mine[:, :, None], flat[None], 0).astype(jnp.bfloat16)
    sent_v = jnp.where(mine[:, :, None], store_upv, 0).astype(jnp.bfloat16)
    got, got_v = lax.psum((sent, sent_v), "rep")
    rank = store_upq.shape[1]
    down = jnp.concatenate(
        [pool_down.reshape(pool, 2 * rank, width), got[:, : 2 * rank]], axis=0
    ).reshape(slots * 2 * rank, width)
    upq = jnp.concatenate([pool_upq, got[:, 2 * rank :]], axis=0).reshape(slots * rank, width)
    upv = jnp.concatenate([pool_upv, got_v], axis=0).reshape(slots * rank, kv_width)

    which = [bit_of(pair_mask[step], bit_total) for step in range(steps)]
    fresh = kv_base.reshape(steps, reqs, 2 * kv_width)
    ids = adapter_ids
    for step in reversed(range(steps)):
        rows = migrating[step]
        payload = jnp.concatenate(
            [
                hidden[step:, rows],
                query_base[step:, rows],
                fresh[step:, rows],
                jnp.broadcast_to(
                    ids[step:, rows][:, :, None], (steps - step, rows.shape[0], LANES)
                ).astype(jnp.bfloat16),
            ],
            axis=2,
        )
        payload = exchange(payload, which[step], bit_total)
        cuts = [width, 2 * width, 2 * width + 2 * kv_width]
        hidden = hidden.at[step:, rows].set(payload[:, :, : cuts[0]])
        query_base = query_base.at[step:, rows].set(payload[:, :, cuts[0] : cuts[1]])
        fresh = fresh.at[step:, rows].set(payload[:, :, cuts[1] : cuts[2]])
        ids = ids.at[step:, rows].set(payload[:, :, cuts[2]].astype(jnp.int32))

    partial_sum = jnp.dot(
        hidden.reshape(steps * reqs, width), down.T, preferred_element_type=jnp.float32
    ).reshape(steps, reqs, slots, 2 * rank)
    picker = ids[:, :, None] == jnp.arange(slots)
    picked = jnp.sum(jnp.where(picker[:, :, :, None], partial_sum, 0.0), axis=2)
    low = lax.psum(picked, "tp").astype(jnp.bfloat16)
    spread = jnp.where(picker[:, :, :, None], low[:, :, None], 0).astype(jnp.bfloat16)
    spread_q = spread[..., :rank].reshape(steps * reqs, slots * rank)
    spread_v = spread[..., rank:].reshape(steps * reqs, slots * rank)
    delta_q = jnp.dot(spread_q, upq, preferred_element_type=jnp.float32)
    delta_v = jnp.dot(spread_v, upv, preferred_element_type=jnp.float32)
    query = (query_base.astype(jnp.float32) + delta_q.reshape(steps, reqs, width)).astype(
        jnp.bfloat16
    )
    new_key = fresh[..., :kv_width]
    new_value = (
        fresh[..., kv_width:].astype(jnp.float32) + delta_v.reshape(steps, reqs, kv_width)
    ).astype(jnp.bfloat16)

    out = attend(query, new_key, new_value, kv_cache, cache_lengths)
    for step in range(steps):
        rows = migrating[step]
        out = out.at[step:, rows].set(exchange(out[step:, rows], which[step], bit_total))
    return out


def solution(mesh):
    return jax.shard_map(
        local,
        mesh=mesh,
        in_specs=(
            P(None, "rep", "tp"),
            P(None, "rep", "tp"),
            P(None, "rep", None, "tp"),
            P("rep", None, None, "tp"),
            P("rep"),
            P(None, "rep"),
            P(None, "rep"),
            P(),
            P(),
            P(None, None, None, "tp"),
            P(None, None, "tp"),
            P(None, None, "tp"),
            P("rep", None, None, "tp"),
            P("rep", None, "tp"),
            P("rep", None, "tp"),
        ),
        out_specs=P(None, "rep", "tp"),
        check_vma=False,
    )
```

time: 1070 us -> 522 us (0.49); the launches traced: 1060 us -> 520 us
  local copies, waits for them, and re-layouts: 691 us -> 175 us
  waiting for transfers between devices: 202 us -> 28.4 us
  Pallas kernels: 0 us -> 117 us
  other arithmetic: 32.3 us -> 148 us
  matrix products: 96 us -> 9.84 us
    slice x24 -> x17, local copies, waits for them, and re-layouts: 407 us -> 14.4 us  [the longest x5 3.5 us: local(): hidden = hidden.at[step:, rows].set(payload[:, :, :cuts[0]])]
    scatter x0 -> x61, other arithmetic: none -> 141 us
    psum x2 -> x1, waiting for transfers between devices: 131 us -> 0.02 us  [local(): got, got_v = lax.psum((sent, sent_v), 'rep')]
    pallas_call x0 -> x1, Pallas kernels: none -> 117 us  [attend(): pl.pallas_call(partial(attend_kernel, group), grid=(reqs // many, heads),...]
    scatter x30 -> x102, local copies, waits for them, and re-layouts: 186 us -> 97.9 us  [the longest x7 105 us: local(): kv_state = kv_state.at[slot_ids].set(moving)]
    dot_general x16 -> x3, matrix products: 68.6 us -> 9.84 us  [the longest x1 4.96 us: local(): delta_q = jnp.dot(spread_q, upq, preferred_element_type=jnp.float32)]
    ppermute x8, waiting for transfers between devices: 71.3 us -> 28.3 us  [swapped(): return lax.ppermute(value, axis, pairs)]
    sub x4 -> x0, matrix products: 27.4 us -> none  [attend(): exp_scores = jnp.exp(scores - row_peak)]
  transfers between devices with their start and end apart: 10 -> 9, of which waited for: 6 -> 8; matrix products, arithmetic and copies ran while one was open for 4% -> 45% of each run, Pallas kernels for 0% -> 0%
where the time goes in v1:
time: 522 us; the launch traced here: 520 us
  local copies, waits for them, and re-layouts  175 us (34%)
  other arithmetic  148 us (28%)
  Pallas kernels  117 us (22%)
  waiting for transfers between devices  28.4 us (5%)
  between operations  21.7 us (4%)
  blocking collectives  10.3 us (2%)
  matrix products  9.84 us (2%)
  starting transfers between devices  8.03 us (2%)
    scatter x60, other arithmetic  127 us
    pallas_call x1, Pallas kernels, attend(): pl.pallas_call(partial(attend_kernel, group), grid=(reqs // many, heads),...  117 us
    scatter x92, local copies, waits for them, and re-layouts  81.9 us
    ppermute x8, waiting for transfers between devices, swapped(): return lax.ppermute(value, axis, pairs)  28.3 us
    unnamed x61, local copies, waits for them, and re-layouts  23.9 us
    scatter x1, other arithmetic, local(): ids = ids.at[step:, rows].set(payload[:, :, cuts[2]].astype(jnp.int32))  14.3 us
  transfers between devices with their start and end apart: 9, of which 8 were waited for; matrix products, arithmetic and copies ran while one was open for 45% of the time, Pallas kernels for 0%

profile of v1, /device:TPU:0, one launch (start us, length us, event | category | flops | bytes accessed | tf_op | source)
XLA Modules:
  0.0 519.9 jit_solution(9520006457738443425)
XLA Ops:
  26.5 6.0 %conditional.8 = (bf16[1,2,9344]{2,1,0:T(2,128)(2,1)}) conditional(s32[]{:T(128)} %bitcast, bf16[1,2,9344]{2,1,0:T(2,128)(2,1)S(1)} %pad_maximum_fusion.4, bf16[1,2,9344]{2,1,0:T(2,128)(2,1)S(1)} %pad_maximum_fusion.4, bf16[1,2,9344]{2,1,0:T(2,128)(2,1)S(1)} %pad_maximum_fusion.4, ...), branch_computations={%region_0.1_spmd, %region_1.2_spmd, %region_2.3_spmd, %region_3.4_... | conditional | bytes 149552 | solution.py:30
  36.7 15.9 %while.19 = (s32[]{:T(128)}, bf16[4,64,4096]{2,1,0:T(8,128)(2,1)}, s32[2,2]{1,0:T(2,128)S(1)}, bf16[2,1,4096]{2,0,1:T(2,128)(2,1)S(1)}, s32[]{:T(128)}, /*index=5*/s32[3]{0:T(128)S(1)}, s32[1]{0:T(128)}, s32[]{:T(128)}) while((s32[]{:T(128)}, bf16[4,64,4096]{2,1,0:T(8,128)(2,1)}, s32[2,2]{1,0:T(2,128)S(1)}, bf16[2,1,4096]{2,0,1:T(2,128)(2,1)S(1)}, ...), condition=%wide.while_cond.2, body=%wide.while_body.2.sunk | while | flops 4115 | bytes 41131 | solution.py:159
  57.3 17.5 %while.22 = (s32[]{:T(128)}, s32[4,64]{1,0:T(4,128)S(1)}, s32[2,2]{1,0:T(2,128)S(1)}, s32[2,1]{1,0:T(2,128)S(1)}, s32[]{:T(128)}, /*index=5*/s32[2]{0:T(128)S(1)}) while((s32[]{:T(128)}, s32[4,64]{1,0:T(4,128)S(1)}, s32[2,2]{1,0:T(2,128)S(1)}, s32[2,1]{1,0:T(2,128)S(1)}, s32[]{:T(128)}, /*index=5*/s32[2]{0:T(128)S(1)}) %tuple.518), condition=%wide.while_cond.5, body=%wide.while_body.5.sunk | while | flops 12 | bytes 171 | solution.py:161
  79.1 11.9 %while.21 = (s32[]{:T(128)}, bf16[4,64,1024]{2,1,0:T(8,128)(2,1)S(1)}, s32[2,2]{1,0:T(2,128)S(1)}, bf16[2,1,1024]{2,0,1:T(2,128)(2,1)S(1)}, s32[]{:T(128)}, /*index=5*/s32[3]{0:T(128)S(1)}, s32[1]{0:T(128)}, s32[]{:T(128)}) while((s32[]{:T(128)}, bf16[4,64,1024]{2,1,0:T(8,128)(2,1)S(1)}, s32[2,2]{1,0:T(2,128)S(1)}, ...), condition=%wide.while_cond.4, body=%wide.while_body.4.sunk | while | flops 1043 | bytes 10411 | solution.py:160
  93.4 12.7 %while.20 = (s32[]{:T(128)}, bf16[4,64,4096]{2,1,0:T(8,128)(2,1)S(1)}, s32[2,2]{1,0:T(2,128)S(1)}, bf16[2,1,4096]{2,0,1:T(2,128)(2,1)S(1)}, s32[]{:T(128)}, /*index=5*/s32[3]{0:T(128)S(1)}, s32[1]{0:T(128)}, s32[]{:T(128)}) while((s32[]{:T(128)}, bf16[4,64,4096]{2,1,0:T(8,128)(2,1)S(1)}, s32[2,2]{1,0:T(2,128)S(1)}, ...), condition=%wide.while_cond.3, body=%wide.while_body.3.sunk | while | flops 4115 | bytes 41131 | solution.py:158
  107.1 8.3 %conditional.9 = (bf16[2,2,9344]{2,1,0:T(2,128)(2,1)}) conditional(s32[]{:T(128)} %bitcast.6, bf16[2,2,9344]{2,1,0:T(2,128)(2,1)S(1)} %pad_maximum_fusion.3, bf16[2,2,9344]{2,1,0:T(2,128)(2,1)S(1)} %pad_maximum_fusion.3, bf16[2,2,9344]{2,1,0:T(2,128)(2,1)S(1)} %pad_maximum_fusion.3, ...), branch_computations={%region_8.9_spmd, %region_9.10_spmd, %region_10.11_spmd, %region_1... | conditional | bytes 299056 | solution.py:30
  121.2 16.4 %while.23 = (s32[]{:T(128)}, bf16[4,64,4096]{2,0,1:T(4,128)(2,1)}, s32[2,2]{1,0:T(2,128)S(1)}, bf16[2,2,4096]{2,1,0:T(2,128)(2,1)S(1)}, s32[]{:T(128)}, /*index=5*/s32[3]{0:T(128)S(1)}, s32[1]{0:T(128)}, s32[]{:T(128)}) while((s32[]{:T(128)}, bf16[4,64,4096]{2,0,1:T(4,128)(2,1)}, s32[2,2]{1,0:T(2,128)S(1)}, bf16[2,2,4096]{2,1,0:T(2,128)(2,1)S(1)}, ...), condition=%wide.while_cond.6, body=%wide.while_body.6.sunk | while | flops 8211 | bytes 82091 | solution.py:159
  137.9 12.6 %while.26 = (s32[]{:T(128)}, s32[4,64]{0,1:T(8,128)S(1)}, s32[2,2]{1,0:T(2,128)S(1)}, s32[2,2]{1,0:T(2,128)S(1)}, s32[]{:T(128)}, /*index=5*/s32[2]{0:T(128)S(1)}) while((s32[]{:T(128)}, s32[4,64]{0,1:T(8,128)S(1)}, s32[2,2]{1,0:T(2,128)S(1)}, s32[2,2]{1,0:T(2,128)S(1)}, s32[]{:T(128)}, /*index=5*/s32[2]{0:T(128)S(1)}) %tuple.523), condition=%wide.while_cond.9, body=%wide.while_body.9.sunk | while | flops 13 | bytes 187 | solution.py:161
  154.6 12.0 %while.25 = (s32[]{:T(128)}, bf16[4,64,1024]{2,0,1:T(4,128)(2,1)S(1)}, s32[2,2]{1,0:T(2,128)S(1)}, bf16[2,2,1024]{2,1,0:T(2,128)(2,1)S(1)}, s32[]{:T(128)}, /*index=5*/s32[3]{0:T(128)S(1)}, s32[1]{0:T(128)}, s32[]{:T(128)}) while((s32[]{:T(128)}, bf16[4,64,1024]{2,0,1:T(4,128)(2,1)S(1)}, s32[2,2]{1,0:T(2,128)S(1)}, ...), condition=%wide.while_cond.8, body=%wide.while_body.8.sunk | while | flops 2067 | bytes 20651 | solution.py:160
  171.2 16.4 %while.24 = (s32[]{:T(128)}, bf16[4,64,4096]{2,0,1:T(4,128)(2,1)}, s32[2,2]{1,0:T(2,128)S(1)}, bf16[2,2,4096]{2,1,0:T(2,128)(2,1)S(1)}, s32[]{:T(128)}, /*index=5*/s32[3]{0:T(128)S(1)}, s32[1]{0:T(128)}, s32[]{:T(128)}) while((s32[]{:T(128)}, bf16[4,64,4096]{2,0,1:T(4,128)(2,1)}, s32[2,2]{1,0:T(2,128)S(1)}, bf16[2,2,4096]{2,1,0:T(2,128)(2,1)S(1)}, ...), condition=%wide.while_cond.7, body=%wide.while_body.7.sunk | while | flops 8211 | bytes 82091 | solution.py:158
  197.7 12.0 %while.27 = (s32[]{:T(128)}, bf16[4,64,4096]{2,0,1:T(4,128)(2,1)S(1)}, s32[2,2]{1,0:T(2,128)S(1)}, bf16[2,3,4096]{2,1,0:T(4,128)(2,1)S(1)}, s32[]{:T(128)}, /*index=5*/s32[3]{0:T(128)S(1)}, s32[1]{0:T(128)}, s32[]{:T(128)}) while((s32[]{:T(128)}, bf16[4,64,4096]{2,0,1:T(4,128)(2,1)S(1)}, s32[2,2]{1,0:T(2,128)S(1)}, ...), condition=%wide.while_cond.10, body=%wide.while_body.10.sunk | while | flops 12307 | bytes 123051 | solution.py:159
  209.8 12.1 %while.29 = (s32[]{:T(128)}, bf16[4,64,1024]{2,0,1:T(4,128)(2,1)S(1)}, s32[2,2]{1,0:T(2,128)S(1)}, bf16[2,3,1024]{2,1,0:T(4,128)(2,1)S(1)}, s32[]{:T(128)}, /*index=5*/s32[3]{0:T(128)S(1)}, s32[1]{0:T(128)}, s32[]{:T(128)}) while((s32[]{:T(128)}, bf16[4,64,1024]{2,0,1:T(4,128)(2,1)S(1)}, s32[2,2]{1,0:T(2,128)S(1)}, ...), condition=%wide.while_cond.12, body=%wide.while_body.12.sunk | while | flops 3091 | bytes 30891 | solution.py:160
  222.0 16.1 %while.28 = (s32[]{:T(128)}, bf16[4,64,4096]{2,0,1:T(4,128)(2,1)}, s32[2,2]{1,0:T(2,128)S(1)}, bf16[2,3,4096]{2,1,0:T(4,128)(2,1)S(1)}, s32[]{:T(128)}, /*index=5*/s32[3]{0:T(128)S(1)}, s32[1]{0:T(128)}, s32[]{:T(128)}) while((s32[]{:T(128)}, bf16[4,64,4096]{2,0,1:T(4,128)(2,1)}, s32[2,2]{1,0:T(2,128)S(1)}, bf16[2,3,4096]{2,1,0:T(4,128)(2,1)S(1)}, ...), condition=%wide.while_cond.11, body=%wide.while_body.11.sunk | while | flops 12307 | bytes 123051 | solution.py:158
  238.1 12.6 %while.30 = (s32[]{:T(128)}, s32[4,64]{0,1:T(8,128)S(1)}, s32[2,2]{1,0:T(2,128)S(1)}, s32[2,3]{1,0:T(2,128)S(1)}, s32[]{:T(128)}, /*index=5*/s32[2]{0:T(128)S(1)}) while((s32[]{:T(128)}, s32[4,64]{0,1:T(8,128)S(1)}, s32[2,2]{1,0:T(2,128)S(1)}, s32[2,3]{1,0:T(2,128)S(1)}, s32[]{:T(128)}, /*index=5*/s32[2]{0:T(128)S(1)}) %tuple.530), condition=%wide.while_cond.13, body=%wide.while_body.13.sunk | while | flops 14 | bytes 207 | solution.py:161
  256.7 6.3 %conditional.11 = (bf16[4,2,9344]{2,1,0:T(2,128)(2,1)}) conditional(s32[]{:T(128)} %bitcast.27, bf16[4,2,9344]{2,0,1:T(4,128)(2,1)S(1)} %pad_maximum_fusion.1, bf16[4,2,9344]{2,0,1:T(4,128)(2,1)S(1)} %pad_maximum_fusion.1, bf16[4,2,9344]{2,0,1:T(4,128)(2,1)S(1)} %pad_maximum_fusion.1, ...), branch_computations={%region_24.25_spmd, %region_25.26_spmd, %region_26.27_spmd, %regio... | conditional | bytes 897072 | solution.py:30
  257.0 6.0 %collective-permute-done.14 = bf16[4,2,9344]{2,1,0:T(2,128)(2,1)} collective-permute-done((bf16[4,2,9344]{2,1,0:T(2,128)(2,1)S(1)}, bf16[4,2,9344]{2,1,0:T(2,128)(2,1)}, u32[]{:S(2)}, u32[]{:S(2)}) %collective-permute-start.14) | collective-permute-done | bytes 149536 | tf_op jit(solution)/shard_map/cond/branch_2_fun/ppermute | solution.py:18
  265.5 14.3 %scatter_custom_fusion.1 = s32[4,64]{0,1:T(8,128)S(1)} fusion(s32[4,64]{0,1:T(8,128)S(1)} %get-tuple-element.186, s32[2]{0:T(128)S(1)} %fusion.21, bf16[4,2,1]{0,1,2:T(2,128)(2,1)S(1)} %copy.221), kind=kCustom, calls=%fused_computation.126 | custom fusion | flops 8 | bytes 1536 | tf_op jit(solution)/shard_map/scatter | solution.py:161
  294.5 10.3 %all-reduce.9 = bf16[4,64,128]{2,1,0:T(8,128)(2,1)S(1)} all-reduce(f32[4,64,128]{2,1,0:T(8,128)S(1)} %fusion.13), channel_id=1, replica_groups=mesh['rep'=16,'tp'=2] {'tp'}, use_global_device_ids=true, to_apply=%region_33.34 | all-reduce | flops 32768 | bytes 196608 | tf_op jit(solution)/shard_map/psum | solution.py:168
  313.4 5.8 %copy-done = bf16[64,128,2,512]{3,2,1,0:T(2,128)(2,1)S(1)} copy-done((bf16[64,128,2,512]{3,2,1,0:T(2,128)(2,1)S(1)}, bf16[64,128,2,512]{3,2,1,0:T(2,128)(2,1)}, u32[]{:S(2)}) %copy-start) | copy-done | bytes 16777240
  319.1 117.3 %attend.1 = bf16[64,4,32,128]{3,2,1,0:T(8,128)(2,1)S(1)} custom-call(s32[64]{0:T(128)S(1)} %copy-done.1, bf16[64,4,32,128]{3,2,1,0:T(8,128)(2,1)S(1)} %bitcast.422, bf16[64,4,32,128]{3,2,1,0:T(8,128)(2,1)S(1)} %bitcast.423, bf16[64,128,4,2,128]{4,3,2,1,0:T(2,128)(2,1)S(1)} %bitcast.421), custom_call_target="tpu_custom_call" | custom-call | flops 1073741824 | bytes 16777216 | tf_op jit(solution)/shard_map/attend/pallas_call | solution.py:81
  453.9 12.0 %while.31 = (s32[]{:T(128)}, bf16[4,64,4096]{2,0,1:T(4,128)(2,1)S(1)}, s32[2,2]{1,0:T(2,128)S(1)}, bf16[2,3,4096]{2,1,0:T(4,128)(2,1)S(1)}, s32[]{:T(128)}, /*index=5*/s32[3]{0:T(128)S(1)}, s32[1]{0:T(128)}, s32[]{:T(128)}) while((s32[]{:T(128)}, bf16[4,64,4096]{2,0,1:T(4,128)(2,1)S(1)}, s32[2,2]{1,0:T(2,128)S(1)}, ...), condition=%wide.while_cond.14, body=%wide.while_body.14.sunk | while | flops 12307 | bytes 123051 | solution.py:185
  470.1 5.0 conditional.14
  475.9 12.4 %while.32 = (s32[]{:T(128)}, bf16[4,64,4096]{2,0,1:T(4,128)(2,1)S(1)}, s32[2,2]{1,0:T(2,128)S(1)}, bf16[2,2,4096]{2,1,0:T(2,128)(2,1)S(1)}, s32[]{:T(128)}, /*index=5*/s32[3]{0:T(128)S(1)}, s32[1]{0:T(128)}, s32[]{:T(128)}) while((s32[]{:T(128)}, bf16[4,64,4096]{2,0,1:T(4,128)(2,1)S(1)}, s32[2,2]{1,0:T(2,128)S(1)}, ...), condition=%wide.while_cond.15, body=%wide.while_body.15.sunk | while | flops 8211 | bytes 82091 | solution.py:185
  496.3 16.5 %while.33 = (s32[]{:T(128)}, bf16[4,64,4096]{2,1,0:T(8,128)(2,1)}, s32[2,2]{1,0:T(2,128)S(1)}, bf16[2,1,4096]{2,0,1:T(2,128)(2,1)}, s32[]{:T(128)}, /*index=5*/s32[3]{0:T(128)S(1)}, s32[1]{0:T(128)}, s32[]{:T(128)}) while((s32[]{:T(128)}, bf16[4,64,4096]{2,1,0:T(8,128)(2,1)}, s32[2,2]{1,0:T(2,128)S(1)}, bf16[2,1,4096]{2,0,1:T(2,128)(2,1)}, ...), condition=%wide.while_cond.16, body=%wide.while_body.16.sunk | while | flops 4115 | bytes 41131 | solution.py:185
  (346 shorter events, 362.7 us)
Async XLA Ops:
  6.5 3.3 copy-start.15
  6.5 276.9 %all-reduce.8.cloned.1.call-start = ((), (), s32[]{:S(2)}) async-start(), calls=%async_computation | async-start | bytes 13107200 | tf_op jit(solution)/shard_map/psum | solution.py:132
  6.5 3.3 copy-start.4
  12.2 3.1 copy-start.9
  16.1 5.1 copy-start.10
  16.2 20.5 %copy-start.6 = (s32[3]{0:T(128)S(1)}, s32[3]{0:T(128)}, u32[]{:S(2)}) copy-start(s32[3]{0:T(128)} %constant.744) | copy-start | bytes 40
  26.5 6.0 %collective-permute-start.1 = (bf16[1,2,9344]{2,1,0:T(2,128)(2,1)S(1)}, bf16[1,2,9344]{2,1,0:T(2,128)(2,1)}, u32[]{:S(2)}, u32[]{:S(2)}) collective-permute-start(bf16[1,2,9344]{2,1,0:T(2,128)(2,1)S(1)} %param.1), channel_id=1, source_target_pairs={{0,4},{2,6},{4,0},{6,2},{8,12},{10,14},{12,8},{14,10},{16,20},{18,... | collective-permute-start | bytes 112136 | tf_op jit(solution)/shard_map/cond/branch_1_fun/ppermute | solution.py:18
  52.6 4.7 copy-start.13
  107.2 8.0 %collective-permute-start.7 = (bf16[2,2,9344]{2,1,0:T(2,128)(2,1)S(1)}, bf16[2,2,9344]{2,1,0:T(2,128)(2,1)}, u32[]{:S(2)}, u32[]{:S(2)}) collective-permute-start(bf16[2,2,9344]{2,1,0:T(2,128)(2,1)S(1)} %param.7), channel_id=1, source_target_pairs={{0,16},{2,18},{4,20},{6,22},{8,24},{10,26},{12,28},{14,30},{16,0},... | collective-permute-start | bytes 224264 | tf_op jit(solution)/shard_map/cond/branch_3_fun/ppermute | solution.py:18
  118.2 3.0 copy-start.7
  118.2 19.6 %copy-start.12 = (s32[2]{0:T(128)S(1)}, s32[2]{0:T(128)}, u32[]{:S(2)}) copy-start(s32[2]{0:T(128)} %constant.837) | copy-start | bytes 28
  187.6 10.1 %copy-start.2 = (bf16[4,64,4096]{2,0,1:T(4,128)(2,1)S(1)}, bf16[4,64,4096]{2,0,1:T(4,128)(2,1)}, u32[]{:S(2)}) copy-start(bf16[4,64,4096]{2,0,1:T(4,128)(2,1)} %get-tuple-element.1325) | copy-start | bytes 6291460
  187.6 10.1 %copy-start.8 = (s32[3]{0:T(128)S(1)}, s32[3]{0:T(128)}, u32[]{:S(2)}) copy-start(s32[3]{0:T(128)} %constant.847) | copy-start | bytes 40
  191.8 46.3 %copy-start.11 = (s32[2]{0:T(128)S(1)}, s32[2]{0:T(128)}, u32[]{:S(2)}) copy-start(s32[2]{0:T(128)} %constant.889) | copy-start | bytes 28
  193.8 1.5 collective-permute-start.8
  256.9 6.1 %collective-permute-start.14 = (bf16[4,2,9344]{2,1,0:T(2,128)(2,1)S(1)}, bf16[4,2,9344]{2,1,0:T(2,128)(2,1)}, u32[]{:S(2)}, u32[]{:S(2)}) collective-permute-start(bf16[4,2,9344]{2,1,0:T(2,128)(2,1)S(1)} %copy.176), channel_id=1, source_target_pairs={{0,8},{2,10},{4,12},{6,14},{8,0},{10,2},{12,4},{14,6},{16,24},{18,... | collective-permute-start | bytes 448520 | tf_op jit(solution)/shard_map/cond/branch_2_fun/ppermute | solution.py:18
  286.6 2.9 copy-start.3
  286.6 3.5 copy-start.16
  312.1 1.3 copy-start.1
  313.4 5.8 %copy-start = (bf16[64,128,2,512]{3,2,1,0:T(2,128)(2,1)S(1)}, bf16[64,128,2,512]{3,2,1,0:T(2,128)(2,1)}, u32[]{:S(2)}) copy-start(bf16[64,128,2,512]{3,2,1,0:T(2,128)(2,1)} %param.50) | copy-start | bytes 50331652
  441.4 4.4 collective-permute-start.18
  451.6 1.4 collective-permute-start.20
  470.2 5.0 collective-permute-start.27
  492.4 3.9 collective-permute-start.29
  (5 other events, 4.5 us)
Sparse Core Ops, SparseCore 0:
  16.3 147.0 all-reduce.7

commit v2 on v1

v2 whole, which is shorter than its diff:
```python
from functools import partial
import math

import jax
import jax.numpy as jnp
from jax import lax
from jax.experimental import pallas as pl
from jax.experimental.pallas import tpu as pltpu
from jax.sharding import PartitionSpec as P

HD = 128
LANES = 128


def swapped(value, axis, bit):
    mask = 2**bit
    pairs = [(source, source ^ mask) for source in range(lax.axis_size(axis))]
    return lax.ppermute(value, axis, pairs)


def bit_of(mask, bit_total):
    which = jnp.zeros((), jnp.int32)
    for bit in range(bit_total):
        which = which + jnp.where(mask == 1 << bit, bit, 0).astype(jnp.int32)
    return which


def exchange(value, which, bit_total):
    branches = [lambda part, bit=bit: swapped(part, "rep", bit) for bit in range(bit_total)]
    return lax.switch(which, branches, value)


def attend_kernel(heads, group, lens_ref, query_ref, fresh_ref, cache_ref, out_ref):
    base = pl.program_id(0) * query_ref.shape[0]
    rows, ctx = query_ref.shape[1], cache_ref.shape[1]
    span = ctx * heads * 2
    extra = fresh_ref.shape[1] // 2
    width = min(span, LANES)
    scale = 1.0 / math.sqrt(HD)
    contract = (((1,), (1,)), ((), ()))
    row = lax.broadcasted_iota(jnp.int32, (rows, width), 0)
    col = lax.broadcasted_iota(jnp.int32, (rows, width), 1)
    own = col % (2 * heads) == 2 * (row // group % heads)
    place = lax.broadcasted_iota(jnp.int32, (1, width), 1) // (2 * heads)
    row_new = lax.broadcasted_iota(jnp.int32, (rows, extra), 0)
    col_new = lax.broadcasted_iota(jnp.int32, (rows, extra), 1)
    seen_new = (col_new % heads == row_new // group % heads) & (
        col_new // heads <= row_new // (group * heads)
    )
    for r in range(query_ref.shape[0]):
        both = cache_ref.at[r].reshape(span, HD)[...]
        query = query_ref[r]
        length = lens_ref[base + r]
        new = lax.dot_general(
            query, fresh_ref[r, :extra], contract, preferred_element_type=jnp.float32
        )
        new = jnp.where(seen_new, new, -1e30)
        scores = lax.dot_general(query, both, contract, preferred_element_type=jnp.float32)
        parts = []
        top = None
        for cut in range(span // width):
            live = own & (place < length - cut * (width // (2 * heads)))
            part = jnp.where(live, scores[:, cut * width : (cut + 1) * width], -1e30)
            parts.append(part)
            top = part if top is None else jnp.maximum(top, part)
        peak = jnp.maximum(
            jnp.max(top, axis=1, keepdims=True), jnp.max(new, axis=1, keepdims=True)
        )
        new = jnp.exp((new - peak) * scale)
        parts = [jnp.exp((part - peak) * scale) for part in parts]
        sums = parts[0]
        for part in parts[1:]:
            sums = sums + part
        total = jnp.sum(sums, axis=1, keepdims=True) + jnp.sum(new, axis=1, keepdims=True)
        inverse = 1.0 / total
        weights = jnp.concatenate(
            [pltpu.roll(part * inverse, 1, 1).astype(jnp.bfloat16) for part in parts], axis=1
        )
        mixed = jnp.dot(weights, both, preferred_element_type=jnp.float32)
        mixed = mixed + jnp.dot(
            (new * inverse).astype(jnp.bfloat16),
            fresh_ref[r, extra:],
            preferred_element_type=jnp.float32,
        )
        out_ref[r] = mixed.astype(out_ref.dtype)


def attend(query, new_key, new_value, kv_cache, lengths):
    steps, reqs = query.shape[:2]
    ctx = kv_cache.shape[1]
    heads = kv_cache.shape[3] // HD
    group = query.shape[2] // (heads * HD)
    rows = steps * heads * group
    query = query.reshape(steps, reqs, heads * group, HD).transpose(1, 0, 2, 3)
    query = query.reshape(reqs, rows, HD)
    extra = -(-steps * heads // 16) * 16
    fresh = jnp.stack([new_key, new_value]).reshape(2, steps, reqs, heads, HD)
    fresh = fresh.transpose(2, 0, 1, 3, 4).reshape(reqs, 2, steps * heads, HD)
    fresh = jnp.pad(fresh, ((0, 0), (0, 0), (0, extra - steps * heads), (0, 0)))
    fresh = fresh.reshape(reqs, 2 * extra, HD)
    cache = kv_cache.reshape(reqs, ctx, 2, heads, HD).transpose(0, 1, 3, 2, 4)
    many = 4 if reqs % 4 == 0 else 1
    out = pl.pallas_call(
        partial(attend_kernel, heads, group),
        grid=(reqs // many,),
        in_specs=[
            pl.BlockSpec(memory_space=pltpu.SMEM),
            pl.BlockSpec((many, rows, HD), lambda r: (r, 0, 0)),
            pl.BlockSpec((many, 2 * extra, HD), lambda r: (r, 0, 0)),
            pl.BlockSpec((many, ctx, heads, 2, HD), lambda r: (r, 0, 0, 0, 0)),
        ],
        out_specs=pl.BlockSpec((many, rows, HD), lambda r: (r, 0, 0)),
        out_shape=jax.ShapeDtypeStruct((reqs, rows, HD), jnp.bfloat16),
        compiler_params=pltpu.CompilerParams(vmem_limit_bytes=24 << 20),
        cost_estimate=pl.CostEstimate(
            flops=8 * reqs * heads * rows * ctx * HD,
            bytes_accessed=2 * kv_cache.size,
            transcendentals=2 * reqs * heads * rows * ctx,
        ),
        name="attend",
    )(lengths, query, fresh, cache)
    out = out.reshape(reqs, steps, heads * group, HD).transpose(1, 0, 2, 3)
    return out.reshape(steps, reqs, -1)


def travel(moved, same, which, bit_total, order):
    steps, entries = moved.shape[:2]
    each = entries // steps
    step_of = jnp.arange(steps)[:, None, None]
    for step in order:
        first = each * step
        came = exchange(moved[step:, first : first + each], which[step], bit_total)
        came = jnp.pad(came, ((step, 0), (0, 0), (0, 0)))
        for j in range(each):
            hit = same[first + j][None, :, None] & (step_of >= step)
            moved = jnp.where(hit, came[:, j : j + 1], moved)
    return moved


def placed(array, moved, hits):
    for entry in range(moved.shape[1]):
        array = jnp.where(hits[entry][None, :, None], moved[:, entry : entry + 1], array)
    return array


def local(
    hidden,
    query_base,
    kv_base,
    kv_cache,
    cache_lengths,
    adapter_ids,
    migrating,
    pair_mask,
    owners,
    pool_down,
    pool_upq,
    pool_upv,
    store_down,
    store_upq,
    store_upv,
):
    steps, reqs, width = hidden.shape
    kv_width = kv_base.shape[3]
    pool = pool_down.shape[0]
    rank = store_upq.shape[1]
    bit_total = lax.axis_size("rep").bit_length() - 1
    me = lax.axis_index("rep")

    mine = owners == me
    got_down, got_upq, got_upv = lax.psum(
        (
            jnp.where(mine[:, None, None], store_down.reshape(1, 2 * rank, width), 0),
            jnp.where(mine[:, None, None], store_upq, 0),
            jnp.where(mine[:, None, None], store_upv, 0),
        ),
        "rep",
    )

    which = [bit_of(pair_mask[step], bit_total) for step in range(steps)]
    rows = migrating.reshape(-1)
    same = rows[:, None] == rows[None, :]
    hits = rows[:, None] == jnp.arange(reqs)[None, :]
    fresh = kv_base.reshape(steps, reqs, 2 * kv_width)
    names = jnp.broadcast_to(
        adapter_ids[:, rows][:, :, None].astype(jnp.bfloat16), (steps, rows.shape[0], LANES)
    )
    moved = jnp.concatenate([hidden[:, rows], query_base[:, rows], fresh[:, rows], names], axis=2)
    moved = travel(moved, same, which, bit_total, reversed(range(steps)))
    cuts = [width, 2 * width, 2 * width + 2 * kv_width]
    hidden = placed(hidden, moved[:, :, : cuts[0]], hits)
    query_base = placed(query_base, moved[:, :, cuts[0] : cuts[1]], hits)
    fresh = placed(fresh, moved[:, :, cuts[1] : cuts[2]], hits)
    ids = placed(
        adapter_ids[:, :, None], moved[:, :, cuts[2] : cuts[2] + 1].astype(jnp.int32), hits
    )

    tokens = hidden.reshape(steps * reqs, width)
    ids = ids.reshape(steps * reqs, 1)

    def picked(down, first):
        many = down.size // (2 * rank * width)
        product = lax.dot_general(
            tokens,
            down.reshape(many * 2 * rank, width),
            (((1,), (1,)), ((), ())),
            preferred_element_type=jnp.float32,
        )
        low = jnp.zeros((steps * reqs, 2 * rank), jnp.float32)
        for one in range(many):
            part = product[:, one * 2 * rank : (one + 1) * 2 * rank]
            low = jnp.where(ids == first + one, part, low)
        return low

    low = jnp.where(ids < pool, picked(pool_down, 0), picked(got_down, pool))
    if lax.axis_size("tp") == 2:
        low = low + lax.ppermute(low, "tp", [(0, 1), (1, 0)])
    else:
        low = lax.psum(low, "tp")
    low = low.astype(jnp.bfloat16)

    def raised(base, up_pool, up_got, half):
        total = base.reshape(steps * reqs, -1).astype(jnp.float32)
        part = low[:, half * rank : (half + 1) * rank]
        for up, first in ((up_pool, 0), (up_got, pool)):
            many = up.shape[0]
            spread = jnp.concatenate(
                [jnp.where(ids == first + one, part, 0) for one in range(many)], axis=1
            )
            total = total + jnp.dot(
                spread, up.reshape(many * rank, -1), preferred_element_type=jnp.float32
            )
        return total.astype(jnp.bfloat16).reshape(steps, reqs, -1)

    query = raised(query_base, pool_upq, got_upq, 0)
    new_value = raised(fresh[:, :, kv_width:], pool_upv, got_upv, 1)
    out = attend(query, fresh[:, :, :kv_width], new_value, kv_cache, cache_lengths)
    moved = travel(out[:, rows], same, which, bit_total, range(steps))
    return placed(out, moved, hits)


def solution(mesh):
    return jax.shard_map(
        local,
        mesh=mesh,
        in_specs=(
            P(None, "rep", "tp"),
            P(None, "rep", "tp"),
            P(None, "rep", None, "tp"),
            P("rep", None, None, "tp"),
            P("rep"),
            P(None, "rep"),
            P(None, "rep"),
            P(),
            P(),
            P(None, None, None, "tp"),
            P(None, None, "tp"),
            P(None, None, "tp"),
            P("rep", None, None, "tp"),
            P("rep", None, "tp"),
            P("rep", None, "tp"),
        ),
        out_specs=P(None, "rep", "tp"),
        check_vma=False,
    )
```

time: 522 us -> 276 us (0.53)
  other arithmetic: 148 us -> 31.8 us
  local copies, waits for them, and re-layouts: 175 us -> 63.8 us
  Pallas kernels: 117 us -> 41.6 us
  waiting for transfers between devices: 28.4 us -> 90.2 us
  blocking collectives: 10.3 us -> 0 us
    scatter x61 -> x0, other arithmetic: 141 us -> none
    scatter x102 -> x0, local copies, waits for them, and re-layouts: 97.9 us -> none
    pallas_call x1, Pallas kernels: 117 us -> 41.6 us  [attend(): pl.pallas_call(partial(attend_kernel, heads, group), grid=(reqs // many,)...]
    psum x1, waiting for transfers between devices: 0.02 us -> 63.7 us  [local(): lax.psum((jnp.where(mine[:, None, None], store_down.reshape(1, 2 * rank,...]
    gather x35 -> x6, local copies, waits for them, and re-layouts: 27.9 us -> 7.71 us  [the longest x1 2.48 us: local(): moved = travel(out[:, rows], same, which, bit_total, range(steps))]
    select_n x4 -> x18, other arithmetic: 4.15 us -> 24 us  [the longest x4 12.3 us: placed(): jnp.where(hits[entry][None, :, None], moved[:, entry:entry + 1], array)]
    psum x1 -> x0, blocking collectives: 10.3 us -> none  [local(): low = lax.psum(picked, 'tp').astype(jnp.bfloat16)]
    and x0 -> x7, local copies, waits for them, and re-layouts: none -> 5.82 us  [travel(): hit = same[first + j][None, :, None] & (step_of >= step)]
  transfers between devices with their start and end apart: 9 -> 10, of which waited for: 8 -> 10; matrix products, arithmetic and copies ran while one was open for 45% -> 21% of each run, Pallas kernels for 0% -> 0%
where the time goes in v2:
time: 276 us; the launch traced here: 271 us
  waiting for transfers between devices  90.2 us (33%)
  local copies, waits for them, and re-layouts  63.8 us (23%)
  Pallas kernels  41.6 us (15%)
  other arithmetic  31.8 us (12%)
  between operations  22.4 us (8%)
  starting transfers between devices  11.6 us (4%)
  matrix products  9.67 us (4%)
    psum x1, waiting for transfers between devices, local(): lax.psum((jnp.where(mine[:, None, None], store_down.reshape(1, 2 * rank,...  63.7 us
    pallas_call x1, Pallas kernels, attend(): pl.pallas_call(partial(attend_kernel, heads, group), grid=(reqs // many,)...  41.6 us
    unnamed x176, local copies, waits for them, and re-layouts  25.4 us
    ppermute x8, waiting for transfers between devices, swapped(): return lax.ppermute(value, axis, pairs)  22.7 us
    select_n x4, other arithmetic, placed(): jnp.where(hits[entry][None, :, None], moved[:, entry:entry + 1], array)  12.3 us
    ppermute x8, starting transfers between devices, swapped(): return lax.ppermute(value, axis, pairs)  10.1 us
    slice x8, local copies, waits for them, and re-layouts, travel(): moved = jnp.where(hit, came[:, j:j + 1], moved)  8.54 us
    and x7, local copies, waits for them, and re-layouts, travel(): hit = same[first + j][None, :, None] & (step_of >= step)  5.82 us
  transfers between devices with their start and end apart: 10, of which 10 were waited for; matrix products, arithmetic and copies ran while one was open for 21% of the time, Pallas kernels for 0%

profile of v2, /device:TPU:0, one launch (start us, length us, event | category | flops | bytes accessed | tf_op | source)
XLA Modules:
  0.0 271.3 jit_solution(1696447406448687963)
XLA Ops:
  7.4 3.6 %broadcast_select_fusion = bf16[4,128,4096]{2,1,0:T(8,128)(2,1)} fusion(pred[4]{0:T(512)(128)(4,1)S(1)} %broadcast_compare_fusion.8, bf16[128,4096]{1,0:T(8,128)(2,1)} %bitcast.253), kind=kLoop, calls=%fused_computation.8 | loop fusion | flops 2097152 | bytes 5242884 | tf_op jit(solution)/shard_map/jit(_where)/select_n | solution.py:173
  26.6 2.0 gather_fusion
  28.6 2.0 gather_fusion.1
  31.6 5.1 %conditional.8 = (bf16[1,2,9344]{2,1,0:T(2,128)(2,1)}) conditional(s32[]{:T(128)} %bitcast.2, bf16[1,2,9344]{2,1,0:T(2,128)(2,1)S(1)} %slice.553, bf16[1,2,9344]{2,1,0:T(2,128)(2,1)S(1)} %slice.553, bf16[1,2,9344]{2,1,0:T(2,128)(2,1)S(1)} %slice.553, bf16[1,2,9344]{2,1,0:T(2,128)(2,1)S(1)} %slice.553), branch_computations={%region_0.1_spmd, %region_1.2_spmd, %region_2.3_spmd, %region_3.4_... | conditional | bytes 149552 | solution.py:30
  31.6 3.0 %collective-permute-start.1 = (bf16[1,2,9344]{2,1,0:T(2,128)(2,1)S(1)}, bf16[1,2,9344]{2,1,0:T(2,128)(2,1)}, u32[]{:S(2)}, u32[]{:S(2)}) collective-permute-start(bf16[1,2,9344]{2,1,0:T(2,128)(2,1)S(1)} %param.1), channel_id=1, source_target_pairs={{0,4},{2,6},{4,0},{6,2},{8,12},{10,14},{12,8},{14,10},{16,20},{18,... | collective-permute-start | bytes 112136 | tf_op jit(solution)/shard_map/cond/branch_1_fun/ppermute | solution.py:18
  34.6 2.0 collective-permute-done.1
  43.9 11.9 %conditional.10 = (bf16[3,2,9344]{2,1,0:T(2,128)(2,1)}) conditional(s32[]{:T(128)} %bitcast.6, bf16[3,2,9344]{2,1,0:T(2,128)(2,1)S(1)} %slice.555, bf16[3,2,9344]{2,1,0:T(2,128)(2,1)S(1)} %slice.555, bf16[3,2,9344]{2,1,0:T(2,128)(2,1)S(1)} %slice.555, bf16[3,2,9344]{2,1,0:T(2,128)(2,1)S(1)} %slice.555), branch_computations={%region_8.9_spmd, %region_9.10_spmd, %region_10.11_spmd, %region_1... | conditional | bytes 448560 | solution.py:30
  44.0 3.1 %collective-permute-start.11 = (bf16[3,2,9344]{2,1,0:T(2,128)(2,1)S(1)}, bf16[3,2,9344]{2,1,0:T(2,128)(2,1)}, u32[]{:S(2)}, u32[]{:S(2)}) collective-permute-start(bf16[3,2,9344]{2,1,0:T(2,128)(2,1)S(1)} %param.11), channel_id=1, source_target_pairs={{0,16},{2,18},{4,20},{6,22},{8,24},{10,26},{12,28},{14,30},{16,0},... | collective-permute-start | bytes 336392 | tf_op jit(solution)/shard_map/cond/branch_3_fun/ppermute | solution.py:18
  47.0 8.7 %collective-permute-done.11 = bf16[3,2,9344]{2,1,0:T(2,128)(2,1)} collective-permute-done((bf16[3,2,9344]{2,1,0:T(2,128)(2,1)S(1)}, bf16[3,2,9344]{2,1,0:T(2,128)(2,1)}, u32[]{:S(2)}, u32[]{:S(2)}) %collective-permute-start.11) | collective-permute-done | bytes 112160 | tf_op jit(solution)/shard_map/cond/branch_3_fun/ppermute | solution.py:18
  93.2 3.2 %select_select_fusion = bf16[4,64,4096]{2,1,0:T(8,128)(2,1)S(1)} fusion(bf16[4,64,4096]{2,1,0:T(8,128)(2,1)} %param.47, pred[64]{0:T(512)(128)(4,1)S(1)} %get-tuple-element.177, pred[64]{0:T(512)(128)(4,1)S(1)} %get-tuple-element.178, pred[64]{0:T(512)(128)(4,1)S(1)} %get-tuple-element.179, pred[64]{0:T(512)(128)(4,1)S(1)} %get-tuple-element.180, ...), kind=kLoop, calls=%fused_computation.17 | loop fusion | flops 8388608 | bytes 4456960 | tf_op jit(solution)/shard_map/jit(_where)/select_n | solution.py:142
  100.6 63.7 %all-reduce.9.cloned.1.call-done = (bf16[512,4096]{1,0:T(8,128)(2,1)}, bf16[256,4096]{1,0:T(8,128)(2,1)}, bf16[256,512]{1,0:T(8,128)(2,1)}) async-done(((bf16[512,4096]{1,0:T(8,128)(2,1)}, bf16[256,4096]{1,0:T(8,128)(2,1)}, bf16[256,512]{1,0:T(8,128)(2,1)}), (bf16[512,4096]{1,0:T(8,128)(2,1)}, bf16[256,4096]{1,0:T(8,128)(2,1)}, bf16[256,512]{1,0:T(8,128)(2,1)})) %all-reduce.9.cloned.1.call-update) | async-done | bytes 6553616 | tf_op jit(solution)/shard_map/psum | solution.py:171
  164.3 4.1 %fusion.47 = f32[256,512]{0,1:T(8,128)S(1)} fusion(bf16[256,4096]{1,0:T(8,128)(2,1)} %bitcast.238, bf16[512,4096]{1,0:T(8,128)(2,1)} %get-tuple-element.85), kind=kOutput, calls=%fused_computation.197 | convolution fusion | flops 1073741824 | bytes 6815744 | tf_op jit(solution)/shard_map/dot_general | solution.py:203
  170.2 3.8 %collective-permute-done.32 = f32[256,128]{0,1:T(8,128)} collective-permute-done((f32[256,128]{0,1:T(8,128)S(1)}, f32[256,128]{0,1:T(8,128)}, u32[]{:S(2)}, u32[]{:S(2)}) %collective-permute-start.32) | collective-permute-done | bytes 131104 | tf_op jit(solution)/shard_map/ppermute | solution.py:217
  177.4 2.0 fusion.9
  186.4 5.8 %copy-done.2 = bf16[64,128,2,512]{3,2,1,0:T(2,128)(2,1)S(1)} copy-done((bf16[64,128,2,512]{3,2,1,0:T(2,128)(2,1)S(1)}, bf16[64,128,2,512]{3,2,1,0:T(2,128)(2,1)}, u32[]{:S(2)}) %copy-start.2) | copy-done | bytes 16777240
  192.2 41.6 %attend.1 = bf16[64,128,128]{2,1,0:T(8,128)(2,1)S(1)} custom-call(s32[64]{0:T(128)S(1)} %copy-done.3, bf16[64,128,128]{2,1,0:T(8,128)(2,1)S(1)} %bitcast.231, bf16[64,32,128]{2,1,0:T(8,128)(2,1)S(1)} %bitcast.233, bf16[64,128,4,2,128]{4,3,2,1,0:T(2,128)(2,1)S(1)} %bitcast.230), custom_call_target="tpu_custom_call" | custom-call | flops 4294967296 | bytes 16777216 | tf_op jit(solution)/shard_map/attend/pallas_call | solution.py:103
  233.8 2.1 reshape.598
  235.9 2.5 gather_fusion.4
  241.5 6.2 %conditional.13 = (bf16[3,2,4096]{2,1,0:T(2,128)(2,1)}) conditional(s32[]{:T(128)} %bitcast.6, bf16[3,2,4096]{2,0,1:T(4,128)(2,1)S(1)} %slice.605, bf16[3,2,4096]{2,0,1:T(4,128)(2,1)S(1)} %slice.605, bf16[3,2,4096]{2,0,1:T(4,128)(2,1)S(1)} %slice.605, bf16[3,2,4096]{2,0,1:T(4,128)(2,1)S(1)} %slice.605), branch_computations={%region_23.24_spmd, %region_24.25_spmd, %region_25.26_spmd, %regio... | conditional | bytes 294960 | solution.py:30
  241.6 2.2 collective-permute-start.23
  243.8 3.9 %collective-permute-done.23 = bf16[3,2,4096]{2,1,0:T(2,128)(2,1)} collective-permute-done((bf16[3,2,4096]{2,1,0:T(2,128)(2,1)S(1)}, bf16[3,2,4096]{2,1,0:T(2,128)(2,1)}, u32[]{:S(2)}, u32[]{:S(2)}) %collective-permute-start.23) | collective-permute-done | bytes 49184 | tf_op jit(solution)/shard_map/cond/branch_3_fun/ppermute | solution.py:18
  252.5 4.0 %conditional.15 = (bf16[1,2,4096]{2,1,0:T(2,128)(2,1)}) conditional(s32[]{:T(128)} %bitcast.2, bf16[1,2,4096]{2,0,1:T(2,128)(2,1)S(1)} %slice.607, bf16[1,2,4096]{2,0,1:T(2,128)(2,1)S(1)} %slice.607, bf16[1,2,4096]{2,0,1:T(2,128)(2,1)S(1)} %slice.607, bf16[1,2,4096]{2,0,1:T(2,128)(2,1)S(1)} %slice.607), branch_computations={%region_31.32_spmd, %region_32.33_spmd, %region_33.34_spmd, %regio... | conditional | bytes 98352 | solution.py:30
  254.1 2.4 collective-permute-done.29
  258.1 6.3 %fusion.7 = bf16[4,64,4096]{2,1,0:T(8,128)(2,1)} fusion(bf16[4,64,4096]{2,0,1:T(4,128)(2,1)} %reshape.598, pred[64]{0:T(512)(128)(4,1)S(1)} %copy-done.22, pred[64]{0:T(512)(128)(4,1)S(1)} %copy-done.24, pred[64]{0:T(512)(128)(4,1)S(1)} %copy-done.26, pred[64]{0:T(512)(128)(4,1)S(1)} %copy-done.29, pred[64]{0:T(512)(128)(4,1)S(1)} %copy-done.32, ...), kind=kLoop, calls=%fused_computation.16 | loop fusion | flops 8388608 | bytes 4456960 | tf_op jit(solution)/shard_map/jit(_where)/select_n | solution.py:142
  (280 shorter events, 86.8 us)
Async XLA Ops:
  6.5 90.0 %copy-start = (bf16[2,2,64,4096]{3,2,1,0:T(8,128)(2,1)S(1)}, bf16[2,2,64,4096]{3,2,1,0:T(8,128)(2,1)}, u32[]{:S(2)}) copy-start(bf16[2,2,64,4096]{3,2,1,0:T(8,128)(2,1)} %param.56) | copy-start | bytes 6291460
  6.5 157.8 %all-reduce.9.cloned.1.call-start = ((), (), s32[]{:S(2)}) async-start(), calls=%async_computation | async-start | bytes 13107200 | tf_op jit(solution)/shard_map/psum | solution.py:171
  13.4 11.8 %copy-start.9 = (bf16[4,64,2,512]{3,2,1,0:T(2,128)(2,1)S(1)}, bf16[4,64,2,512]{3,2,1,0:T(2,128)(2,1)}, u32[]{:S(2)}) copy-start(bf16[4,64,2,512]{3,2,1,0:T(2,128)(2,1)} %param.49) | copy-start | bytes 1572868
  31.6 5.0 %collective-permute-start.1 = (bf16[1,2,9344]{2,1,0:T(2,128)(2,1)S(1)}, bf16[1,2,9344]{2,1,0:T(2,128)(2,1)}, u32[]{:S(2)}, u32[]{:S(2)}) collective-permute-start(bf16[1,2,9344]{2,1,0:T(2,128)(2,1)S(1)} %param.1), channel_id=1, source_target_pairs={{0,4},{2,6},{4,0},{6,2},{8,12},{10,14},{12,8},{14,10},{16,20},{18,... | collective-permute-start | bytes 112136 | tf_op jit(solution)/shard_map/cond/branch_1_fun/ppermute | solution.py:18
  39.9 1.5 collective-permute-start.4
  43.5 17.1 %copy-start.48 = (pred[4,8]{1,0:T(4,128)(4,1)}, pred[4,8]{1,0:T(4,128)(4,1)S(1)}, u32[]{:S(2)}) copy-start(pred[4,8]{1,0:T(4,128)(4,1)S(1)} %get-tuple-element.189) | copy-start | bytes 100
  43.5 17.1 %copy-start.50 = (pred[4,8]{1,0:T(4,128)(4,1)}, pred[4,8]{1,0:T(4,128)(4,1)S(1)}, u32[]{:S(2)}) copy-start(pred[4,8]{1,0:T(4,128)(4,1)S(1)} %get-tuple-element.188) | copy-start | bytes 100
  43.8 16.8 %copy-start.39 = (pred[8]{0:T(512)(128)(4,1)S(1)}, pred[8]{0:T(512)(128)(4,1)}, u32[]{:S(2)}) copy-start(pred[8]{0:T(512)(128)(4,1)} %get-tuple-element.168) | copy-start | bytes 28
  43.8 16.8 %copy-start.41 = (pred[8]{0:T(512)(128)(4,1)S(1)}, pred[8]{0:T(512)(128)(4,1)}, u32[]{:S(2)}) copy-start(pred[8]{0:T(512)(128)(4,1)} %get-tuple-element.169) | copy-start | bytes 28
  44.0 11.8 %collective-permute-start.11 = (bf16[3,2,9344]{2,1,0:T(2,128)(2,1)S(1)}, bf16[3,2,9344]{2,1,0:T(2,128)(2,1)}, u32[]{:S(2)}, u32[]{:S(2)}) collective-permute-start(bf16[3,2,9344]{2,1,0:T(2,128)(2,1)S(1)} %param.11), channel_id=1, source_target_pairs={{0,16},{2,18},{4,20},{6,22},{8,24},{10,26},{12,28},{14,30},{16,0},... | collective-permute-start | bytes 336392 | tf_op jit(solution)/shard_map/cond/branch_3_fun/ppermute | solution.py:18
  57.6 1.6 collective-permute-start.12
  82.4 10.8 %copy-start.13 = (bf16[4,1,4096]{2,0,1:T(4,128)(2,1)S(1)}, bf16[4,1,4096]{2,0,1:T(4,128)(2,1)}, u32[]{:S(2)}) copy-start(bf16[4,1,4096]{2,0,1:T(4,128)(2,1)} %copy.261) | copy-start | bytes 98308
  82.4 10.8 %copy-start.14 = (bf16[4,1,4096]{2,0,1:T(4,128)(2,1)S(1)}, bf16[4,1,4096]{2,0,1:T(4,128)(2,1)}, u32[]{:S(2)}) copy-start(bf16[4,1,4096]{2,0,1:T(4,128)(2,1)} %copy.262) | copy-start | bytes 98308
  168.6 5.4 %collective-permute-start.32 = (f32[256,128]{0,1:T(8,128)S(1)}, f32[256,128]{0,1:T(8,128)}, u32[]{:S(2)}, u32[]{:S(2)}) collective-permute-start(f32[256,128]{0,1:T(8,128)S(1)} %fusion.13), channel_id=1, source_target_pairs={{0,1},{1,0},{2,3},{3,2},{4,5},{5,4},{6,7},{7,6},{8,9},{9,8},{10,11... | collective-permute-start | bytes 393224 | tf_op jit(solution)/shard_map/ppermute | solution.py:217
  235.9 13.0 %copy-start.44 = (pred[4,8]{0,1:T(8,128)(4,1)S(1)}, pred[4,8]{0,1:T(8,128)(4,1)}, u32[]{:S(2)}) copy-start(pred[4,8]{0,1:T(8,128)(4,1)} %copy.112) | copy-start | bytes 100
  235.9 13.0 %copy-start.45 = (pred[4,8]{0,1:T(8,128)(4,1)S(1)}, pred[4,8]{0,1:T(8,128)(4,1)}, u32[]{:S(2)}) copy-start(pred[4,8]{0,1:T(8,128)(4,1)} %copy.135) | copy-start | bytes 100
  238.4 13.5 %copy-start.52 = (pred[4,8]{0,1:T(8,128)(4,1)S(1)}, pred[4,8]{0,1:T(8,128)(4,1)}, u32[]{:S(2)}) copy-start(pred[4,8]{0,1:T(8,128)(4,1)} %copy.111) | copy-start | bytes 100
  238.4 13.5 %copy-start.53 = (pred[4,8]{0,1:T(8,128)(4,1)S(1)}, pred[4,8]{0,1:T(8,128)(4,1)}, u32[]{:S(2)}) copy-start(pred[4,8]{0,1:T(8,128)(4,1)} %copy.140) | copy-start | bytes 100
  238.5 1.5 collective-permute-start.16
  241.1 16.3 %copy-start.62 = (pred[4,8]{0,1:T(8,128)(4,1)S(1)}, pred[4,8]{0,1:T(8,128)(4,1)}, u32[]{:S(2)}) copy-start(pred[4,8]{0,1:T(8,128)(4,1)} %copy.110) | copy-start | bytes 100
  241.1 16.3 %copy-start.63 = (pred[4,8]{0,1:T(8,128)(4,1)S(1)}, pred[4,8]{0,1:T(8,128)(4,1)}, u32[]{:S(2)}) copy-start(pred[4,8]{0,1:T(8,128)(4,1)} %copy.145) | copy-start | bytes 100
  241.6 6.1 %collective-permute-start.23 = (bf16[3,2,4096]{2,1,0:T(2,128)(2,1)S(1)}, bf16[3,2,4096]{2,1,0:T(2,128)(2,1)}, u32[]{:S(2)}, u32[]{:S(2)}) collective-permute-start(bf16[3,2,4096]{2,1,0:T(2,128)(2,1)S(1)} %copy.134), channel_id=1, source_target_pairs={{0,16},{2,18},{4,20},{6,22},{8,24},{10,26},{12,28},{14,30},{16,0},... | collective-permute-start | bytes 147464 | tf_op jit(solution)/shard_map/cond/branch_3_fun/ppermute | solution.py:18
  249.4 1.4 collective-permute-start.24
  252.6 3.9 %collective-permute-start.29 = (bf16[1,2,4096]{2,1,0:T(2,128)(2,1)S(1)}, bf16[1,2,4096]{2,1,0:T(2,128)(2,1)}, u32[]{:S(2)}, u32[]{:S(2)}) collective-permute-start(bf16[1,2,4096]{2,1,0:T(2,128)(2,1)S(1)} %copy.142), channel_id=1, source_target_pairs={{0,4},{2,6},{4,0},{6,2},{8,12},{10,14},{12,8},{14,10},{16,20},{18,... | collective-permute-start | bytes 49160 | tf_op jit(solution)/shard_map/cond/branch_1_fun/ppermute | solution.py:18
  (53 other events, 280.4 us)
Sparse Core Ops, SparseCore 0:
  13.5 150.7 all-reduce.8

commit v3 on v2

--- a/solution.py
+++ b/solution.py
@@ -30,8 +30,15 @@
     return lax.switch(which, branches, value)
 
 
-def attend_kernel(heads, group, lens_ref, query_ref, fresh_ref, cache_ref, out_ref):
-    base = pl.program_id(0) * query_ref.shape[0]
+def exchange_open(value, which, bit_total):
+    came = swapped(value, "rep", 0)
+    for bit in range(1, bit_total):
+        came = jnp.where(which == bit, swapped(value, "rep", bit), came)
+    return came
+
+
+def attend_kernel(heads, group, order_ref, lens_ref, query_ref, fresh_ref, cache_ref, out_ref):
+    base = order_ref[pl.program_id(0)] * query_ref.shape[0]
     rows, ctx = query_ref.shape[1], cache_ref.shape[1]
     span = ctx * heads * 2
     extra = fresh_ref.shape[1] // 2
@@ -85,7 +92,7 @@
         out_ref[r] = mixed.astype(out_ref.dtype)
 
 
-def attend(query, new_key, new_value, kv_cache, lengths):
+def attend(query, new_key, new_value, kv_cache, lengths, moving):
     steps, reqs = query.shape[:2]
     ctx = kv_cache.shape[1]
     heads = kv_cache.shape[3] // HD
@@ -99,37 +106,51 @@
     fresh = jnp.pad(fresh, ((0, 0), (0, 0), (0, extra - steps * heads), (0, 0)))
     fresh = fresh.reshape(reqs, 2 * extra, HD)
     cache = kv_cache.reshape(reqs, ctx, 2, heads, HD).transpose(0, 1, 3, 2, 4)
-    many = 4 if reqs % 4 == 0 else 1
-    out = pl.pallas_call(
-        partial(attend_kernel, heads, group),
-        grid=(reqs // many,),
-        in_specs=[
-            pl.BlockSpec(memory_space=pltpu.SMEM),
-            pl.BlockSpec((many, rows, HD), lambda r: (r, 0, 0)),
-            pl.BlockSpec((many, 2 * extra, HD), lambda r: (r, 0, 0)),
-            pl.BlockSpec((many, ctx, heads, 2, HD), lambda r: (r, 0, 0, 0, 0)),
-        ],
-        out_specs=pl.BlockSpec((many, rows, HD), lambda r: (r, 0, 0)),
-        out_shape=jax.ShapeDtypeStruct((reqs, rows, HD), jnp.bfloat16),
-        compiler_params=pltpu.CompilerParams(vmem_limit_bytes=24 << 20),
-        cost_estimate=pl.CostEstimate(
-            flops=8 * reqs * heads * rows * ctx * HD,
-            bytes_accessed=2 * kv_cache.size,
-            transcendentals=2 * reqs * heads * rows * ctx,
-        ),
-        name="attend",
-    )(lengths, query, fresh, cache)
-    out = out.reshape(reqs, steps, heads * group, HD).transpose(1, 0, 2, 3)
-    return out.reshape(steps, reqs, -1)
-
-
-def travel(moved, same, which, bit_total, order):
+
+    def call(order, many):
+        count = order.shape[0]
+        block = lambda r, order_ref, lens_ref: (order_ref[r], 0, 0)
+        wide = lambda r, order_ref, lens_ref: (order_ref[r], 0, 0, 0, 0)
+        out = pl.pallas_call(
+            partial(attend_kernel, heads, group),
+            grid_spec=pltpu.PrefetchScalarGridSpec(
+                num_scalar_prefetch=2,
+                grid=(count,),
+                in_specs=[
+                    pl.BlockSpec((many, rows, HD), block),
+                    pl.BlockSpec((many, 2 * extra, HD), block),
+                    pl.BlockSpec((many, ctx, heads, 2, HD), wide),
+                ],
+                out_specs=pl.BlockSpec((many, rows, HD), lambda r, *_: (r, 0, 0)),
+            ),
+            out_shape=jax.ShapeDtypeStruct((count * many, rows, HD), jnp.bfloat16),
+            compiler_params=pltpu.CompilerParams(vmem_limit_bytes=48 << 20),
+            cost_estimate=pl.CostEstimate(
+                flops=64 * count * many * heads * rows * ctx * HD,
+                bytes_accessed=8 * count * many * ctx * heads * HD,
+                transcendentals=2 * count * many * heads * rows * ctx,
+            ),
+            name="attend",
+        )(order, lengths, query, fresh, cache)
+        out = out.reshape(count * many, steps, heads * group, HD).transpose(1, 0, 2, 3)
+        return out.reshape(steps, count * many, -1)
+
+    leaving = call(moving, 1)
+    many = 4 if reqs % 16 == 0 else 1
+    blocks = reqs // many
+    parts = 4 if blocks % 4 == 0 else 1
+    orders = jnp.arange(blocks, dtype=jnp.int32).reshape(parts, -1)
+    staying = [call(orders[part], many) for part in range(parts)]
+    return leaving, jnp.concatenate(staying, axis=1)
+
+
+def travel(moved, same, which, bit_total, order, swap):
     steps, entries = moved.shape[:2]
     each = entries // steps
     step_of = jnp.arange(steps)[:, None, None]
     for step in order:
         first = each * step
-        came = exchange(moved[step:, first : first + each], which[step], bit_total)
+        came = swap(moved[step:, first : first + each], which[step], bit_total)
         came = jnp.pad(came, ((step, 0), (0, 0), (0, 0)))
         for j in range(each):
             hit = same[first + j][None, :, None] & (step_of >= step)
@@ -186,7 +207,7 @@
         adapter_ids[:, rows][:, :, None].astype(jnp.bfloat16), (steps, rows.shape[0], LANES)
     )
     moved = jnp.concatenate([hidden[:, rows], query_base[:, rows], fresh[:, rows], names], axis=2)
-    moved = travel(moved, same, which, bit_total, reversed(range(steps)))
+    moved = travel(moved, same, which, bit_total, reversed(range(steps)), exchange)
     cuts = [width, 2 * width, 2 * width + 2 * kv_width]
     hidden = placed(hidden, moved[:, :, : cuts[0]], hits)
     query_base = placed(query_base, moved[:, :, cuts[0] : cuts[1]], hits)
@@ -234,8 +255,10 @@
 
     query = raised(query_base, pool_upq, got_upq, 0)
     new_value = raised(fresh[:, :, kv_width:], pool_upv, got_upv, 1)
-    out = attend(query, fresh[:, :, :kv_width], new_value, kv_cache, cache_lengths)
-    moved = travel(out[:, rows], same, which, bit_total, range(steps))
+    leaving, out = attend(
+        query, fresh[:, :, :kv_width], new_value, kv_cache, cache_lengths, rows
+    )
+    moved = travel(leaving, same, which, bit_total, range(steps), exchange_open)
     return placed(out, moved, hits)
 
 

time: 276 us -> 282 us (1.022)
  local copies, waits for them, and re-layouts: 63.8 us -> 43.4 us
  Pallas kernels: 41.6 us -> 56.6 us
  starting transfers between devices: 11.6 us -> 22.3 us
  waiting for transfers between devices: 90.2 us -> 98.6 us
  other arithmetic: 31.8 us -> 24.9 us
    pallas_call x1 -> x5, Pallas kernels: 41.6 us -> 56.6 us  [call(): pl.pallas_call(partial(attend_kernel, heads, group), grid_spec=pltpu.Pref...]
    ppermute x8 -> x20, starting transfers between devices: 10.1 us -> 20.7 us  [swapped(): return lax.ppermute(value, axis, pairs)]
    unnamed x176 -> x162, local copies, waits for them, and re-layouts: 25.4 us -> 16 us
    psum x1, waiting for transfers between devices: 63.7 us -> 68.2 us  [local(): lax.psum((jnp.where(mine[:, None, None], store_down.reshape(1, 2 * rank,...]
    ppermute x8 -> x20, waiting for transfers between devices: 22.7 us -> 26.6 us  [swapped(): return lax.ppermute(value, axis, pairs)]
    slice x8 -> x4, local copies, waits for them, and re-layouts: 8.54 us -> 4.71 us  [travel(): moved = jnp.where(hit, came[:, j:j + 1], moved)]
  transfers between devices with their start and end apart: 10 -> 22, of which waited for: 10 -> 6; matrix products, arithmetic and copies ran while one was open for 21% -> 17% of each run, Pallas kernels for 0% -> 17%
where the time goes in v3:
time: 282 us; the launch traced here: 277 us
  waiting for transfers between devices  98.6 us (35%)
  Pallas kernels  56.6 us (20%)
  local copies, waits for them, and re-layouts  43.4 us (15%)
  other arithmetic  24.9 us (9%)
  between operations  23.1 us (8%)
  starting transfers between devices  22.3 us (8%)
  matrix products  8.43 us (3%)
    psum x1, waiting for transfers between devices, local(): lax.psum((jnp.where(mine[:, None, None], store_down.reshape(1, 2 * rank,...  68.2 us
    pallas_call x5, Pallas kernels, call(): pl.pallas_call(partial(attend_kernel, heads, group), grid_spec=pltpu.Pref...  56.6 us
    ppermute x20, waiting for transfers between devices, swapped(): return lax.ppermute(value, axis, pairs)  26.6 us
    ppermute x20, starting transfers between devices, swapped(): return lax.ppermute(value, axis, pairs)  20.7 us
    unnamed x162, local copies, waits for them, and re-layouts  16 us
    select_n x4, other arithmetic, placed(): jnp.where(hits[entry][None, :, None], moved[:, entry:entry + 1], array)  9.54 us
  transfers between devices with their start and end apart: 22, of which 6 were waited for; matrix products, arithmetic and copies ran while one was open for 17% of the time, Pallas kernels for 17%

profile of v3, /device:TPU:0, one launch (start us, length us, event | category | flops | bytes accessed | tf_op | source)
XLA Modules:
  0.0 277.4 jit_solution(6188238712307420207)
XLA Ops:
  7.4 3.6 %broadcast_select_fusion = bf16[4,128,4096]{2,1,0:T(8,128)(2,1)} fusion(pred[4]{0:T(512)(128)(4,1)S(1)} %broadcast_compare_fusion.8, bf16[128,4096]{1,0:T(8,128)(2,1)} %bitcast.305), kind=kLoop, calls=%fused_computation.7 | loop fusion | flops 2097152 | bytes 5242884 | tf_op jit(solution)/shard_map/jit(_where)/select_n | solution.py:194
  25.0 2.0 gather_fusion
  27.0 2.0 gather_fusion.1
  30.0 6.1 %conditional.4 = (bf16[1,2,9344]{2,1,0:T(2,128)(2,1)}) conditional(s32[]{:T(128)} %bitcast.12, bf16[1,2,9344]{2,1,0:T(2,128)(2,1)S(1)} %slice.519, bf16[1,2,9344]{2,1,0:T(2,128)(2,1)S(1)} %slice.519, bf16[1,2,9344]{2,1,0:T(2,128)(2,1)S(1)} %slice.519, bf16[1,2,9344]{2,1,0:T(2,128)(2,1)S(1)} %slice.519), branch_computations={%region_0.1_spmd, %region_1.2_spmd, %region_2.3_spmd, %region_3.4_... | conditional | bytes 149552 | solution.py:30
  30.0 3.1 %collective-permute-start.2 = (bf16[1,2,9344]{2,1,0:T(2,128)(2,1)S(1)}, bf16[1,2,9344]{2,1,0:T(2,128)(2,1)}, u32[]{:S(2)}, u32[]{:S(2)}) collective-permute-start(bf16[1,2,9344]{2,1,0:T(2,128)(2,1)S(1)} %param.2), channel_id=1, source_target_pairs={{0,8},{2,10},{4,12},{6,14},{8,0},{10,2},{12,4},{14,6},{16,24},{18,... | collective-permute-start | bytes 112136 | tf_op jit(solution)/shard_map/cond/branch_2_fun/ppermute | solution.py:18
  33.1 3.0 %collective-permute-done.2 = bf16[1,2,9344]{2,1,0:T(2,128)(2,1)} collective-permute-done((bf16[1,2,9344]{2,1,0:T(2,128)(2,1)S(1)}, bf16[1,2,9344]{2,1,0:T(2,128)(2,1)}, u32[]{:S(2)}, u32[]{:S(2)}) %collective-permute-start.2) | collective-permute-done | bytes 37408 | tf_op jit(solution)/shard_map/cond/branch_2_fun/ppermute | solution.py:18
  42.1 11.8 %conditional.6 = (bf16[3,2,9344]{2,1,0:T(2,128)(2,1)}) conditional(s32[]{:T(128)} %bitcast.10, bf16[3,2,9344]{2,1,0:T(2,128)(2,1)S(1)} %slice.521, bf16[3,2,9344]{2,1,0:T(2,128)(2,1)S(1)} %slice.521, bf16[3,2,9344]{2,1,0:T(2,128)(2,1)S(1)} %slice.521, bf16[3,2,9344]{2,1,0:T(2,128)(2,1)S(1)} %slice.521), branch_computations={%region_8.9_spmd, %region_9.10_spmd, %region_10.11_spmd, %region_1... | conditional | bytes 448560 | solution.py:30
  42.1 3.0 %collective-permute-start.11 = (bf16[3,2,9344]{2,1,0:T(2,128)(2,1)S(1)}, bf16[3,2,9344]{2,1,0:T(2,128)(2,1)}, u32[]{:S(2)}, u32[]{:S(2)}) collective-permute-start(bf16[3,2,9344]{2,1,0:T(2,128)(2,1)S(1)} %param.11), channel_id=1, source_target_pairs={{0,16},{2,18},{4,20},{6,22},{8,24},{10,26},{12,28},{14,30},{16,0},... | collective-permute-start | bytes 336392 | tf_op jit(solution)/shard_map/cond/branch_3_fun/ppermute | solution.py:18
  45.1 8.7 %collective-permute-done.11 = bf16[3,2,9344]{2,1,0:T(2,128)(2,1)} collective-permute-done((bf16[3,2,9344]{2,1,0:T(2,128)(2,1)S(1)}, bf16[3,2,9344]{2,1,0:T(2,128)(2,1)}, u32[]{:S(2)}, u32[]{:S(2)}) %collective-permute-start.11) | collective-permute-done | bytes 112160 | tf_op jit(solution)/shard_map/cond/branch_3_fun/ppermute | solution.py:18
  55.8 14.0 %conditional.7 = (bf16[4,2,9344]{2,1,0:T(2,128)(2,1)}) conditional(s32[]{:T(128)} %bitcast.9, bf16[4,2,9344]{2,1,0:T(2,128)(2,1)S(1)} %slice.522, bf16[4,2,9344]{2,1,0:T(2,128)(2,1)S(1)} %slice.522, bf16[4,2,9344]{2,1,0:T(2,128)(2,1)S(1)} %slice.522, bf16[4,2,9344]{2,1,0:T(2,128)(2,1)S(1)} %slice.522), branch_computations={%region_12.13_spmd, %region_13.14_spmd, %region_14.15_spmd, %regio... | conditional | bytes 598064 | solution.py:30
  56.3 13.4 %collective-permute-done.15 = bf16[4,2,9344]{2,1,0:T(2,128)(2,1)} collective-permute-done((bf16[4,2,9344]{2,1,0:T(2,128)(2,1)S(1)}, bf16[4,2,9344]{2,1,0:T(2,128)(2,1)}, u32[]{:S(2)}, u32[]{:S(2)}) %collective-permute-start.15) | collective-permute-done | bytes 149536 | tf_op jit(solution)/shard_map/cond/branch_3_fun/ppermute | solution.py:18
  95.3 3.3 %select_select_fusion = bf16[4,64,4096]{2,1,0:T(8,128)(2,1)S(1)} fusion(bf16[4,64,4096]{2,1,0:T(8,128)(2,1)} %param.31, pred[64]{0:T(512)(128)(4,1)S(1)} %get-tuple-element.145, pred[64]{0:T(512)(128)(4,1)S(1)} %get-tuple-element.146, pred[64]{0:T(512)(128)(4,1)S(1)} %get-tuple-element.147, pred[64]{0:T(512)(128)(4,1)S(1)} %get-tuple-element.148, ...), kind=kLoop, calls=%fused_computation.16 | loop fusion | flops 8388608 | bytes 4456960 | tf_op jit(solution)/shard_map/jit(_where)/select_n | solution.py:163
  102.6 68.2 %all-reduce.9.cloned.1.call-done = (bf16[512,4096]{1,0:T(8,128)(2,1)}, bf16[256,4096]{1,0:T(8,128)(2,1)}, bf16[256,512]{1,0:T(8,128)(2,1)}) async-done(((bf16[512,4096]{1,0:T(8,128)(2,1)}, bf16[256,4096]{1,0:T(8,128)(2,1)}, bf16[256,512]{1,0:T(8,128)(2,1)}), (bf16[512,4096]{1,0:T(8,128)(2,1)}, bf16[256,4096]{1,0:T(8,128)(2,1)}, bf16[256,512]{1,0:T(8,128)(2,1)})) %all-reduce.9.cloned.1.call-update) | async-done | bytes 6553616 | tf_op jit(solution)/shard_map/psum | solution.py:192
  170.8 4.1 %fusion.52 = f32[256,512]{0,1:T(8,128)S(1)} fusion(bf16[256,4096]{1,0:T(8,128)(2,1)} %bitcast.291, bf16[512,4096]{1,0:T(8,128)(2,1)} %get-tuple-element.49), kind=kOutput, calls=%fused_computation.208 | convolution fusion | flops 1073741824 | bytes 6815744 | tf_op jit(solution)/shard_map/dot_general | solution.py:224
  176.6 3.8 %collective-permute-done.16 = f32[256,128]{0,1:T(8,128)S(1)} collective-permute-done((f32[256,128]{0,1:T(8,128)S(1)}, f32[256,128]{0,1:T(8,128)S(1)}, u32[]{:S(2)}, u32[]{:S(2)}) %collective-permute-start.16) | collective-permute-done | bytes 131104 | tf_op jit(solution)/shard_map/ppermute | solution.py:238
  182.3 2.1 convolution_add_fusion.1
  186.5 8.3 %attend.5 = bf16[8,128,128]{2,1,0:T(8,128)(2,1)S(1)} custom-call(s32[8]{0:T(128)S(1)} %eq.200.order_ref, s32[64]{0:T(128)S(1)} %copy-done.8, bf16[64,128,128]{2,1,0:T(8,128)(2,1)S(1)} %bitcast.267, bf16[64,32,128]{2,1,0:T(8,128)(2,1)S(1)} %bitcast.272, bf16[64,128,4,2,128]{4,3,2,1,0:T(2,128)(2,1)} %bitcast.282), custom_call_target="tpu_custom_call" | custom-call | flops 4294967296 | bytes 4194304 | tf_op jit(solution)/shard_map/attend/pallas_call | solution.py:114
  195.0 2.2 collective-permute-start.17
  199.4 12.0 %attend.6 = bf16[16,128,128]{2,1,0:T(8,128)(2,1)S(1)} custom-call(s32[4]{0:T(128)S(1)} %get-tuple-element.126.order_ref, s32[64]{0:T(128)S(1)} %copy-done.8, bf16[64,128,128]{2,1,0:T(8,128)(2,1)S(1)} %bitcast.268, bf16[64,32,128]{2,1,0:T(8,128)(2,1)S(1)} %bitcast.273, bf16[64,128,4,2,128]{4,3,2,1,0:T(2,128)(2,1)} %bitcast.283), custom_call_target="tpu_custom_call" | custom-call | flops 8589934592 | bytes 8388608 | tf_op jit(solution)/shard_map/attend/pallas_call | solution.py:114
  214.6 12.0 %attend.7 = bf16[16,128,128]{2,1,0:T(8,128)(2,1)S(1)} custom-call(s32[4]{0:T(128)S(1)} %get-tuple-element.129.order_ref, s32[64]{0:T(128)S(1)} %copy-done.8, bf16[64,128,128]{2,1,0:T(8,128)(2,1)S(1)} %bitcast.269, bf16[64,32,128]{2,1,0:T(8,128)(2,1)S(1)} %bitcast.274, bf16[64,128,4,2,128]{4,3,2,1,0:T(2,128)(2,1)} %bitcast.284), custom_call_target="tpu_custom_call" | custom-call | flops 8589934592 | bytes 8388608 | tf_op jit(solution)/shard_map/attend/pallas_call | solution.py:114
  227.3 2.2 collective-permute-start.25
  231.8 12.0 %attend.8 = bf16[16,128,128]{2,1,0:T(8,128)(2,1)S(1)} custom-call(s32[4]{0:T(128)S(1)} %get-tuple-element.128.order_ref, s32[64]{0:T(128)S(1)} %copy-done.8, bf16[64,128,128]{2,1,0:T(8,128)(2,1)S(1)} %bitcast.270, bf16[64,32,128]{2,1,0:T(8,128)(2,1)S(1)} %bitcast.275, bf16[64,128,4,2,128]{4,3,2,1,0:T(2,128)(2,1)} %bitcast.285), custom_call_target="tpu_custom_call" | custom-call | flops 8589934592 | bytes 8388608 | tf_op jit(solution)/shard_map/attend/pallas_call | solution.py:114
  247.8 12.3 %attend.9 = bf16[16,128,128]{2,1,0:T(8,128)(2,1)S(1)} custom-call(s32[4]{0:T(128)S(1)} %get-tuple-element.127.order_ref, s32[64]{0:T(128)S(1)} %copy-done.8, bf16[64,128,128]{2,1,0:T(8,128)(2,1)S(1)} %bitcast.271, bf16[64,32,128]{2,1,0:T(8,128)(2,1)S(1)} %bitcast.276, bf16[64,128,4,2,128]{4,3,2,1,0:T(2,128)(2,1)} %bitcast.286), custom_call_target="tpu_custom_call" | custom-call | flops 8589934592 | bytes 8388608 | tf_op jit(solution)/shard_map/attend/pallas_call | solution.py:114
  265.9 4.2 %fusion.7 = bf16[4,64,4096]{2,1,0:T(8,128)(2,1)} fusion(bf16[4,16,4096]{2,1,0:T(8,128)(2,1)S(1)} %copy.89, bf16[4,16,4096]{2,1,0:T(8,128)(2,1)S(1)} %copy-done.13, bf16[4,16,4096]{2,1,0:T(8,128)(2,1)S(1)} %copy.87, bf16[4,16,4096]{2,1,0:T(8,128)(2,1)S(1)} %copy.86, pred[64]{0:T(512)(128)(4,1)S(1)} %get-tuple-element.145, ...), kind=kLoop, calls=%fused_computation.15 | loop fusion | flops 16777216 | bytes 4456960 | tf_op jit(solution)/shard_map/jit(_where)/select_n | solution.py:163
  (299 shorter events, 70.0 us)
Async XLA Ops:
  6.5 92.1 %copy-start = (bf16[2,2,64,4096]{3,2,1,0:T(8,128)(2,1)S(1)}, bf16[2,2,64,4096]{3,2,1,0:T(8,128)(2,1)}, u32[]{:S(2)}) copy-start(bf16[2,2,64,4096]{3,2,1,0:T(8,128)(2,1)} %param.40) | copy-start | bytes 6291460
  6.5 164.2 %all-reduce.9.cloned.1.call-start = ((), (), s32[]{:S(2)}) async-start(), calls=%async_computation | async-start | bytes 13107200 | tf_op jit(solution)/shard_map/psum | solution.py:192
  30.0 6.1 %collective-permute-start.2 = (bf16[1,2,9344]{2,1,0:T(2,128)(2,1)S(1)}, bf16[1,2,9344]{2,1,0:T(2,128)(2,1)}, u32[]{:S(2)}, u32[]{:S(2)}) collective-permute-start(bf16[1,2,9344]{2,1,0:T(2,128)(2,1)S(1)} %param.2), channel_id=1, source_target_pairs={{0,8},{2,10},{4,12},{6,14},{8,0},{10,2},{12,4},{14,6},{16,24},{18,... | collective-permute-start | bytes 112136 | tf_op jit(solution)/shard_map/cond/branch_2_fun/ppermute | solution.py:18
  37.2 34.0 %copy-start.33 = (pred[8]{0:T(512)(128)(4,1)}, pred[8]{0:T(512)(128)(4,1)S(1)}, u32[]{:S(2)}) copy-start(pred[8]{0:T(512)(128)(4,1)S(1)} %get-tuple-element.136) | copy-start | bytes 28
  38.9 1.5 collective-permute-start.4
  42.1 11.7 %collective-permute-start.11 = (bf16[3,2,9344]{2,1,0:T(2,128)(2,1)S(1)}, bf16[3,2,9344]{2,1,0:T(2,128)(2,1)}, u32[]{:S(2)}, u32[]{:S(2)}) collective-permute-start(bf16[3,2,9344]{2,1,0:T(2,128)(2,1)S(1)} %param.11), channel_id=1, source_target_pairs={{0,16},{2,18},{4,20},{6,22},{8,24},{10,26},{12,28},{14,30},{16,0},... | collective-permute-start | bytes 336392 | tf_op jit(solution)/shard_map/cond/branch_3_fun/ppermute | solution.py:18
  55.8 13.8 %collective-permute-start.15 = (bf16[4,2,9344]{2,1,0:T(2,128)(2,1)S(1)}, bf16[4,2,9344]{2,1,0:T(2,128)(2,1)}, u32[]{:S(2)}, u32[]{:S(2)}) collective-permute-start(bf16[4,2,9344]{2,1,0:T(2,128)(2,1)S(1)} %param.15), channel_id=1, source_target_pairs={{0,16},{2,18},{4,20},{6,22},{8,24},{10,26},{12,28},{14,30},{16,0},... | collective-permute-start | bytes 448520 | tf_op jit(solution)/shard_map/cond/branch_3_fun/ppermute | solution.py:18
  175.1 5.3 %collective-permute-start.16 = (f32[256,128]{0,1:T(8,128)S(1)}, f32[256,128]{0,1:T(8,128)S(1)}, u32[]{:S(2)}, u32[]{:S(2)}) collective-permute-start(f32[256,128]{0,1:T(8,128)S(1)} %fusion.13), channel_id=1, source_target_pairs={{0,1},{1,0},{2,3},{3,2},{4,5},{5,4},{6,7},{7,6},{8,9},{9,8},{10,11... | collective-permute-start | bytes 393224 | tf_op jit(solution)/shard_map/ppermute | solution.py:238
  195.0 16.5 %collective-permute-start.17 = (bf16[4,2,4096]{2,0,1:T(4,128)(2,1)S(1)}, bf16[4,2,4096]{2,0,1:T(4,128)(2,1)S(1)}, u32[]{:S(2)}, u32[]{:S(2)}) collective-permute-start(bf16[4,2,4096]{2,0,1:T(4,128)(2,1)S(1)} %slice.568), channel_id=1, source_target_pairs={{0,16},{2,18},{4,20},{6,22},{8,24},{10,26},{12,28},{14,30},{16,0},... | collective-permute-start | bytes 196616 | tf_op jit(solution)/shard_map/ppermute | solution.py:18
  197.2 14.3 %collective-permute-start.18 = (bf16[4,2,4096]{2,0,1:T(4,128)(2,1)S(1)}, bf16[4,2,4096]{2,0,1:T(4,128)(2,1)S(1)}, u32[]{:S(2)}, u32[]{:S(2)}) collective-permute-start(bf16[4,2,4096]{2,0,1:T(4,128)(2,1)S(1)} %slice.568), channel_id=1, source_target_pairs={{0,8},{2,10},{4,12},{6,14},{8,0},{10,2},{12,4},{14,6},{16,24},{18,... | collective-permute-start | bytes 196616 | tf_op jit(solution)/shard_map/ppermute | solution.py:18
  197.9 13.5 %collective-permute-start.19 = (bf16[4,2,4096]{2,0,1:T(4,128)(2,1)S(1)}, bf16[4,2,4096]{2,0,1:T(4,128)(2,1)S(1)}, u32[]{:S(2)}, u32[]{:S(2)}) collective-permute-start(bf16[4,2,4096]{2,0,1:T(4,128)(2,1)S(1)} %slice.568), channel_id=1, source_target_pairs={{0,4},{2,6},{4,0},{6,2},{8,12},{10,14},{12,8},{14,10},{16,20},{18,... | collective-permute-start | bytes 196616 | tf_op jit(solution)/shard_map/ppermute | solution.py:18
  199.4 12.1 %collective-permute-start.20 = (bf16[4,2,4096]{2,0,1:T(4,128)(2,1)S(1)}, bf16[4,2,4096]{2,0,1:T(4,128)(2,1)S(1)}, u32[]{:S(2)}, u32[]{:S(2)}) collective-permute-start(bf16[4,2,4096]{2,0,1:T(4,128)(2,1)S(1)} %slice.568), channel_id=1, source_target_pairs={{0,2},{2,0},{4,6},{6,4},{8,10},{10,8},{12,14},{14,12},{16,18},{18,... | collective-permute-start | bytes 196616 | tf_op jit(solution)/shard_map/ppermute | solution.py:18
  212.0 14.7 %collective-permute-start.21 = (bf16[3,2,4096]{2,0,1:T(4,128)(2,1)S(1)}, bf16[3,2,4096]{2,0,1:T(4,128)(2,1)S(1)}, u32[]{:S(2)}, u32[]{:S(2)}) collective-permute-start(bf16[3,2,4096]{2,0,1:T(4,128)(2,1)S(1)} %slice.571), channel_id=1, source_target_pairs={{0,16},{2,18},{4,20},{6,22},{8,24},{10,26},{12,28},{14,30},{16,0},... | collective-permute-start | bytes 147464 | tf_op jit(solution)/shard_map/ppermute | solution.py:18
  213.3 13.4 %collective-permute-start.22 = (bf16[3,2,4096]{2,0,1:T(4,128)(2,1)S(1)}, bf16[3,2,4096]{2,0,1:T(4,128)(2,1)S(1)}, u32[]{:S(2)}, u32[]{:S(2)}) collective-permute-start(bf16[3,2,4096]{2,0,1:T(4,128)(2,1)S(1)} %slice.571), channel_id=1, source_target_pairs={{0,8},{2,10},{4,12},{6,14},{8,0},{10,2},{12,4},{14,6},{16,24},{18,... | collective-permute-start | bytes 147464 | tf_op jit(solution)/shard_map/ppermute | solution.py:18
  214.1 12.6 %collective-permute-start.23 = (bf16[3,2,4096]{2,0,1:T(4,128)(2,1)S(1)}, bf16[3,2,4096]{2,0,1:T(4,128)(2,1)S(1)}, u32[]{:S(2)}, u32[]{:S(2)}) collective-permute-start(bf16[3,2,4096]{2,0,1:T(4,128)(2,1)S(1)} %slice.571), channel_id=1, source_target_pairs={{0,4},{2,6},{4,0},{6,2},{8,12},{10,14},{12,8},{14,10},{16,20},{18,... | collective-permute-start | bytes 147464 | tf_op jit(solution)/shard_map/ppermute | solution.py:18
  214.6 12.1 %collective-permute-start.24 = (bf16[3,2,4096]{2,0,1:T(4,128)(2,1)S(1)}, bf16[3,2,4096]{2,0,1:T(4,128)(2,1)S(1)}, u32[]{:S(2)}, u32[]{:S(2)}) collective-permute-start(bf16[3,2,4096]{2,0,1:T(4,128)(2,1)S(1)} %slice.571), channel_id=1, source_target_pairs={{0,2},{2,0},{4,6},{6,4},{8,10},{10,8},{12,14},{14,12},{16,18},{18,... | collective-permute-start | bytes 147464 | tf_op jit(solution)/shard_map/ppermute | solution.py:18
  227.3 16.5 %collective-permute-start.25 = (bf16[2,2,4096]{2,0,1:T(2,128)(2,1)S(1)}, bf16[2,2,4096]{2,0,1:T(2,128)(2,1)S(1)}, u32[]{:S(2)}, u32[]{:S(2)}) collective-permute-start(bf16[2,2,4096]{2,0,1:T(2,128)(2,1)S(1)} %slice.572), channel_id=1, source_target_pairs={{0,16},{2,18},{4,20},{6,22},{8,24},{10,26},{12,28},{14,30},{16,0},... | collective-permute-start | bytes 98312 | tf_op jit(solution)/shard_map/ppermute | solution.py:18
  229.5 14.3 %collective-permute-start.26 = (bf16[2,2,4096]{2,0,1:T(2,128)(2,1)S(1)}, bf16[2,2,4096]{2,0,1:T(2,128)(2,1)S(1)}, u32[]{:S(2)}, u32[]{:S(2)}) collective-permute-start(bf16[2,2,4096]{2,0,1:T(2,128)(2,1)S(1)} %slice.572), channel_id=1, source_target_pairs={{0,8},{2,10},{4,12},{6,14},{8,0},{10,2},{12,4},{14,6},{16,24},{18,... | collective-permute-start | bytes 98312 | tf_op jit(solution)/shard_map/ppermute | solution.py:18
  230.3 13.6 %collective-permute-start.27 = (bf16[2,2,4096]{2,0,1:T(2,128)(2,1)S(1)}, bf16[2,2,4096]{2,0,1:T(2,128)(2,1)S(1)}, u32[]{:S(2)}, u32[]{:S(2)}) collective-permute-start(bf16[2,2,4096]{2,0,1:T(2,128)(2,1)S(1)} %slice.572), channel_id=1, source_target_pairs={{0,4},{2,6},{4,0},{6,2},{8,12},{10,14},{12,8},{14,10},{16,20},{18,... | collective-permute-start | bytes 98312 | tf_op jit(solution)/shard_map/ppermute | solution.py:18
  231.8 12.1 %collective-permute-start.28 = (bf16[2,2,4096]{2,0,1:T(2,128)(2,1)S(1)}, bf16[2,2,4096]{2,0,1:T(2,128)(2,1)S(1)}, u32[]{:S(2)}, u32[]{:S(2)}) collective-permute-start(bf16[2,2,4096]{2,0,1:T(2,128)(2,1)S(1)} %slice.572), channel_id=1, source_target_pairs={{0,2},{2,0},{4,6},{6,4},{8,10},{10,8},{12,14},{14,12},{16,18},{18,... | collective-permute-start | bytes 98312 | tf_op jit(solution)/shard_map/ppermute | solution.py:18
  245.2 18.9 %collective-permute-start.29 = (bf16[1,2,4096]{2,0,1:T(2,128)(2,1)}, bf16[1,2,4096]{2,0,1:T(2,128)(2,1)}, u32[]{:S(2)}, u32[]{:S(2)}) collective-permute-start(bf16[1,2,4096]{2,0,1:T(2,128)(2,1)} %slice.573), channel_id=1, source_target_pairs={{0,16},{2,18},{4,20},{6,22},{8,24},{10,26},{12,28},{14,30},{16,0},... | collective-permute-start | bytes 49160 | tf_op jit(solution)/shard_map/ppermute | solution.py:18
  246.5 17.7 %collective-permute-start.30 = (bf16[1,2,4096]{2,0,1:T(2,128)(2,1)}, bf16[1,2,4096]{2,0,1:T(2,128)(2,1)}, u32[]{:S(2)}, u32[]{:S(2)}) collective-permute-start(bf16[1,2,4096]{2,0,1:T(2,128)(2,1)} %slice.573), channel_id=1, source_target_pairs={{0,8},{2,10},{4,12},{6,14},{8,0},{10,2},{12,4},{14,6},{16,24},{18,... | collective-permute-start | bytes 49160 | tf_op jit(solution)/shard_map/ppermute | solution.py:18
  247.3 16.9 %collective-permute-start.31 = (bf16[1,2,4096]{2,0,1:T(2,128)(2,1)}, bf16[1,2,4096]{2,0,1:T(2,128)(2,1)}, u32[]{:S(2)}, u32[]{:S(2)}) collective-permute-start(bf16[1,2,4096]{2,0,1:T(2,128)(2,1)} %slice.573), channel_id=1, source_target_pairs={{0,4},{2,6},{4,0},{6,2},{8,12},{10,14},{12,8},{14,10},{16,20},{18,... | collective-permute-start | bytes 49160 | tf_op jit(solution)/shard_map/ppermute | solution.py:18
  247.8 16.3 %collective-permute-start.32 = (bf16[1,2,4096]{2,0,1:T(2,128)(2,1)}, bf16[1,2,4096]{2,0,1:T(2,128)(2,1)}, u32[]{:S(2)}, u32[]{:S(2)}) collective-permute-start(bf16[1,2,4096]{2,0,1:T(2,128)(2,1)} %slice.573), channel_id=1, source_target_pairs={{0,2},{2,0},{4,6},{6,4},{8,10},{10,8},{12,14},{14,12},{16,18},{18,... | collective-permute-start | bytes 49160 | tf_op jit(solution)/shard_map/ppermute | solution.py:18
  (62 other events, 363.1 us)
Sparse Core Ops, SparseCore 0:
  13.6 157.1 all-reduce.8
